TPU v7x, 128 devices: a whole 4x4x4 slice. The times are simulated.
128 devices in a mesh: seq: 16 (over y, x_lo, core), head: 8 (over x_hi, z).
Axes of the slice: x: 4 (x_hi: 2, x_lo: 2; x = x_hi * 2 + x_lo), y: 4, z: 4, core: 2. Of those that a mesh axis runs over, the one named last changes fastest.
Arguments:
- q_prompt: bfloat16 [2048, 8192], P('seq', 'head'), may hold values from -200 to 200
- k_prompt: bfloat16 [2048, 1024], P('seq', 'head'), may hold values from -6 to 6
- v_prompt: bfloat16 [2048, 1024], P('seq', 'head'), may hold values from -6 to 6
- do_prompt: bfloat16 [2048, 8192], P('seq', 'head'), may hold values from -6 to 6
- q_resp: bfloat16 [4096, 8192], P('seq', 'head'), may hold values from -200 to 200
- k_resp: bfloat16 [4096, 1024], P('seq', 'head'), may hold values from -6 to 6
- v_resp: bfloat16 [4096, 1024], P('seq', 'head'), may hold values from -6 to 6
- do_resp: bfloat16 [4096, 8192], P('seq', 'head'), may hold values from -6 to 6
- resp_lengths: int32 [16, 4], P('seq'), may hold values from 1 to 128, 256 in all within a row
- resp_prompt: int32 [16, 4], P('seq'), may hold values from 0 to 1
- w_query: bfloat16 [5120, 8192], P(None, 'head'), may hold values from -0.75 to 0.75
- w_key: bfloat16 [5120, 1024], P(None, 'head'), may hold values from -0.5 to 0.5
- w_value: bfloat16 [5120, 1024], P(None, 'head'), may hold values from -0.5 to 0.5
Outputs:
- dx_prompt: bfloat16 [2048, 5120], P('seq', 'head')
- dx_resp: bfloat16 [4096, 5120], P('seq', 'head')
Inputs may be any that keep to these rules, and one draw needn't show every extreme that they name: `resp_lengths`: each row sums to 256; its largest entry is 128.
All inputs are finite; a program needn't handle non-finite values.
Results may differ from a plain program's by a relative error of at most 0.024.
Values may be sent and summed in bfloat16 or wider, within the bound.
A program may use at most 128 MiB of HBM per device.

v0:
```python
import math

import jax
import jax.numpy as jnp
from jax import lax
from jax.sharding import PartitionSpec as P

HEADS = 64
KV_HEADS = 8
HEAD_DIM = 128
PROMPTS = 2


NEG = -1e30


def piece_stats(scores, grads, visible):
    top = jnp.max(jnp.where(visible, scores, NEG), axis=-1)
    weight = jnp.where(visible, jnp.exp(scores - top[..., None]), 0.0)
    return (top, jnp.sum(weight, axis=-1), jnp.sum(weight * grads, axis=-1))


def merge_stats(first, second):
    top = jnp.maximum(first[0], second[0])
    fa = jnp.exp(first[0] - top)
    fb = jnp.exp(second[0] - top)
    return (top, first[1] * fa + second[1] * fb, first[2] * fa + second[2] * fb)


def shards(
    q_prompt,
    k_prompt,
    v_prompt,
    do_prompt,
    q_resp,
    k_resp,
    v_resp,
    do_resp,
    resp_lengths,
    resp_prompt,
    w_query,
    w_key,
    w_value,
):
    seq_count = lax.axis_size("seq")
    me_seq = lax.axis_index("seq")
    pdev = q_prompt.shape[0]
    rdev = q_resp.shape[0]
    rows = pdev + rdev
    kv_local = k_prompt.shape[1] // HEAD_DIM
    group = HEADS // KV_HEADS
    total = pdev * seq_count
    prompt_len = total // PROMPTS
    scale = 1.0 / math.sqrt(HEAD_DIM)
    block = math.gcd(total, 512)
    blocks = total // block
    q_all = jnp.concatenate([q_prompt, q_resp], axis=0).reshape(rows, kv_local, group, HEAD_DIM)
    do_all = jnp.concatenate([do_prompt, do_resp], axis=0).reshape(rows, kv_local, group, HEAD_DIM)
    ends = jnp.cumsum(resp_lengths[0])
    place = jnp.arange(rdev, dtype=jnp.int32)
    segment = jnp.sum((place[:, None] >= ends[None, :]).astype(jnp.int32), axis=1)
    slots = jnp.arange(resp_lengths.shape[1], dtype=jnp.int32)
    tok_prompt = jnp.sum(
        jnp.where(segment[:, None] == slots[None, :], resp_prompt[0][None, :], 0), axis=1
    )
    own_rows = me_seq * pdev + jnp.arange(pdev, dtype=jnp.int32)
    query_prompt = jnp.concatenate([own_rows // prompt_len, tok_prompt])
    query_place = jnp.concatenate([own_rows, jnp.full((rdev,), total, jnp.int32)])

    def visible(start, count):
        key_rows = start + jnp.arange(count, dtype=jnp.int32)
        seen = (query_prompt[:, None] == (key_rows // prompt_len)[None, :]) & (
            key_rows[None, :] <= query_place[:, None]
        )
        return seen[None, None]

    def scores_of(keys, values):
        scores = (
            jnp.einsum("rhgd,khd->hgrk", q_all, keys, preferred_element_type=jnp.float32) * scale
        )
        grads = jnp.einsum("rhgd,khd->hgrk", do_all, values, preferred_element_type=jnp.float32)
        return (scores, grads)

    keys_mine = k_prompt.reshape(pdev, kv_local, HEAD_DIM)
    values_mine = v_prompt.reshape(pdev, kv_local, HEAD_DIM)
    start_stats = (
        jnp.full((kv_local, group, rows), NEG, jnp.float32),
        jnp.zeros((kv_local, group, rows), jnp.float32),
        jnp.zeros((kv_local, group, rows), jnp.float32),
    )
    keys = lax.all_gather(keys_mine, "seq", axis=0, tiled=True)
    values = lax.all_gather(values_mine, "seq", axis=0, tiled=True)
    scores, grads = scores_of(keys, values)
    stats = merge_stats(
        start_stats, piece_stats(scores, grads, visible(jnp.int32(0), keys.shape[0]))
    )
    keys_all, values_all = (
        lax.all_gather(keys_mine, "seq", axis=0, tiled=True),
        lax.all_gather(values_mine, "seq", axis=0, tiled=True),
    )
    q_r = q_all[pdev:]
    do_r = do_all[pdev:]
    keys_r = k_resp.reshape(rdev, kv_local, HEAD_DIM)
    values_r = v_resp.reshape(rdev, kv_local, HEAD_DIM)
    local_seen = ((segment[:, None] == segment[None, :]) & (place[None, :] <= place[:, None]))[
        None, None
    ]
    scores_rr = (
        jnp.einsum("rhgd,khd->hgrk", q_r, keys_r, preferred_element_type=jnp.float32) * scale
    )
    grads_rr = jnp.einsum("rhgd,khd->hgrk", do_r, values_r, preferred_element_type=jnp.float32)
    local = piece_stats(scores_rr, grads_rr, local_seen)
    pad_top = jnp.full((kv_local, group, pdev), NEG, jnp.float32)
    pad_zero = jnp.zeros((kv_local, group, pdev), jnp.float32)
    local = (
        jnp.concatenate([pad_top, local[0]], axis=2),
        jnp.concatenate([pad_zero, local[1]], axis=2),
        jnp.concatenate([pad_zero, local[2]], axis=2),
    )
    top, norm_total, weighted = merge_stats(stats, local)
    mean_term = weighted / norm_total

    def grad_step(dq_sum, pieces, start):
        keys, values = pieces
        scores, grads = scores_of(keys, values)
        prob = (
            jnp.where(visible(start, keys.shape[0]), jnp.exp(scores - top[..., None]), 0.0)
            / norm_total[..., None]
        )
        dscore = (prob * (grads - mean_term[..., None]) * scale).astype(jnp.bfloat16)
        prob_b = prob.astype(jnp.bfloat16)
        dq_sum = dq_sum + jnp.einsum(
            "hgrk,khd->rhgd", dscore, keys, preferred_element_type=jnp.float32
        )
        dkey = jnp.einsum("hgrk,rhgd->khd", dscore, q_all, preferred_element_type=jnp.float32)
        dvalue = jnp.einsum("hgrk,rhgd->khd", prob_b, do_all, preferred_element_type=jnp.float32)
        return (dq_sum, (dkey, dvalue))

    key_blocks = keys_all.reshape(blocks, block, kv_local, HEAD_DIM)
    value_blocks = values_all.reshape(blocks, block, kv_local, HEAD_DIM)
    starts = jnp.arange(blocks, dtype=jnp.int32) * block

    def visit(state, item):
        return grad_step(state, (item[0], item[1]), item[2])

    dq_sum, (dkey_blocks, dvalue_blocks) = lax.scan(
        visit,
        jnp.zeros((rows, kv_local, group, HEAD_DIM), jnp.float32),
        (key_blocks, value_blocks, starts),
    )
    dkey_whole = dkey_blocks.reshape(total, kv_local, HEAD_DIM)
    dvalue_whole = dvalue_blocks.reshape(total, kv_local, HEAD_DIM)
    top_r = top[:, :, pdev:]
    prob_rr = (
        jnp.where(local_seen, jnp.exp(scores_rr - top_r[..., None]), 0.0)
        / norm_total[:, :, pdev:][..., None]
    )
    dscore_rr = (prob_rr * (grads_rr - mean_term[:, :, pdev:][..., None]) * scale).astype(
        jnp.bfloat16
    )
    prob_rr_b = prob_rr.astype(jnp.bfloat16)
    dq_resp = dq_sum[pdev:] + jnp.einsum(
        "hgqk,khd->qhgd", dscore_rr, keys_r, preferred_element_type=jnp.float32
    )
    dk_resp = jnp.einsum("hgqk,qhgd->khd", dscore_rr, q_r, preferred_element_type=jnp.float32)
    dv_resp = jnp.einsum("hgqk,qhgd->khd", prob_rr_b, do_r, preferred_element_type=jnp.float32)

    def input_term(dquery, dkey, dvalue, count):
        dquery = dquery.astype(jnp.bfloat16).reshape(count, kv_local * group * HEAD_DIM)
        dkey = dkey.astype(jnp.bfloat16).reshape(count, kv_local * HEAD_DIM)
        dvalue = dvalue.astype(jnp.bfloat16).reshape(count, kv_local * HEAD_DIM)
        term = jnp.einsum("rc,dc->rd", dquery, w_query, preferred_element_type=jnp.float32)
        term = term + jnp.einsum("rc,dc->rd", dkey, w_key, preferred_element_type=jnp.float32)
        return term + jnp.einsum("rc,dc->rd", dvalue, w_value, preferred_element_type=jnp.float32)

    term_resp = input_term(dq_resp, dk_resp, dv_resp, rdev)
    dk_prompt, dv_prompt = (
        lax.psum_scatter(
            dkey_whole.astype(jnp.bfloat16), "seq", scatter_dimension=0, tiled=True
        ).astype(jnp.float32),
        lax.psum_scatter(
            dvalue_whole.astype(jnp.bfloat16), "seq", scatter_dimension=0, tiled=True
        ).astype(jnp.float32),
    )
    term_prompt = input_term(dq_sum[:pdev], dk_prompt, dv_prompt, pdev)
    both = lax.psum_scatter(
        jnp.concatenate([term_prompt, term_resp], axis=0).astype(jnp.bfloat16),
        "head",
        scatter_dimension=1,
        tiled=True,
    ).astype(jnp.float32)
    both = both.astype(jnp.bfloat16)
    dx_prompt = both[:pdev]
    dx_resp = both[pdev:]
    return (dx_prompt, dx_resp)


def solution(mesh):
    return jax.shard_map(
        shards,
        mesh=mesh,
        in_specs=(
            P("seq", "head"),
            P("seq", "head"),
            P("seq", "head"),
            P("seq", "head"),
            P("seq", "head"),
            P("seq", "head"),
            P("seq", "head"),
            P("seq", "head"),
            P("seq", None),
            P("seq", None),
            P(None, "head"),
            P(None, "head"),
            P(None, "head"),
        ),
        out_specs=(P("seq", "head"), P("seq", "head")),
        check_vma=False,
    )
```

profile of v0, /device:TPU:0, one launch (start us, length us, event | category | flops | bytes accessed | tf_op | source)
XLA Modules:
  0.0 401.2 jit_solution(6563481558880888225)
XLA Ops:
  11.5 22.5 %all-gather = bf16[2048,128]{1,0:T(8,128)(2,1)S(1)} all-gather(bf16[128,128]{1,0:T(8,128)(2,1)} %param.16), channel_id=2, replica_groups=mesh['seq'=16,'head'=8] {'seq'}, dimensions={0}, use_global_device_ids=true | all-gather | bytes 557056 | tf_op jit(solution)/shard_map/all_gather | solution.py:98
  36.9 20.0 %all-gather.1 = bf16[2048,128]{1,0:T(8,128)(2,1)} all-gather(bf16[128,128]{1,0:T(8,128)(2,1)S(1)} %copy-done.22), channel_id=3, replica_groups=mesh['seq'=16,'head'=8] {'seq'}, dimensions={0}, use_global_device_ids=true | all-gather | bytes 557056 | tf_op jit(solution)/shard_map/all_gather | solution.py:99
  62.7 10.7 %fusion.38 = (f32[8,384]{1,0:T(8,128)S(1)}, f32[384,8,2048]{2,0,1:T(8,128)}) fusion(pred[384,2048]{1,0:T(8,128)(4,1)S(1)} %fusion.44, bf16[384,8,128]{0,2,1:T(8,128)(2,1)S(1)} %bitcast.377, bf16[2048,128]{1,0:T(8,128)(2,1)S(1)} %all-gather), kind=kOutput, calls=%fused_computation.47 | convolution fusion | flops 1629484032 | bytes 27275264 | tf_op jit(solution)/shard_map/rhgd,khd->hgrk/dot_general | solution.py:79
  73.4 11.8 %fusion.41 = f32[8,384]{1,0:T(8,128)S(1)} fusion(f32[384,8,2048]{2,0,1:T(8,128)} %get-tuple-element.318, f32[8,384]{1,0:T(8,128)S(1)} %get-tuple-element.317, pred[384,2048]{1,0:T(8,128)(4,1)S(1)} %fusion.44), kind=kLoop, calls=%fused_computation.50 | loop fusion | flops 25162752 | bytes 25976832 | tf_op jit(solution)/shard_map/reduce_sum | solution.py:20
  85.3 12.9 %fusion.37 = f32[8,384]{1,0:T(8,128)S(1)} fusion(f32[384,8,2048]{2,0,1:T(8,128)} %get-tuple-element.318, f32[8,384]{1,0:T(8,128)S(1)} %get-tuple-element.317, pred[384,2048]{1,0:T(8,128)(4,1)S(1)} %fusion.44, bf16[384,8,128]{0,2,1:T(8,128)(2,1)S(1)} %bitcast.380, bf16[2048,128]{1,0:T(8,128)(2,1)S(1)} %copy-done.15), kind=kOutput, calls=%fused_computation.44 | convolution fusion | flops 1642066944 | bytes 27287552 | tf_op jit(solution)/shard_map/rhgd,khd->hgrk/dot_general | solution.py:81
  102.2 73.0 %while.17 = (s32[]{:T(128)}, f32[384,1,8,128]{0,3,2,1:T(8,128)}, bf16[4,512,1,128]{3,1,2,0:T(8,128)(2,1)}, bf16[4,512,1,128]{3,1,2,0:T(8,128)(2,1)}, bf16[4,512,...) while((s32[]{:T(128)}, f32[384,1,8,128]{0,3,2,1:T(8,128)}, ...), condition=%wide.region_10.11_spmd.clone, body=%wide.region_9.10_spmd.clone.sunk | while | flops 2035097600 | bytes 105390912 | solution.py:146
  107.5 4.8 %fusion.155 = bf16[8,384,512]{1,2,0:T(8,128)(2,1)} fusion(f32[8,384]{1,0:T(8,128)S(1)} %bitcast.393, f32[8,384]{1,0:T(8,128)S(1)} %bitcast.391, f32[8,384]{1,0:T(8,128)S(1)} %bitcast.389, f32[512,384,8]{1,0,2:T(8,128)S(1)} %fusion.154, pred[384,512]{0,1:T(8,128)(4,1)S(1)} %compare_and_fusion.2, bf16[384,1,8,128]{3,0,2,1:T(8,128)(2,1)S(1)} %copy-done.13, ...), kind=kOutput, calls=%fused_computation.8.clone.1 | convolution fusion | flops 415236096 | bytes 10588672 | tf_op jit(solution)/shard_map/while/body/eval_jaxpr/rhgd,khd->hgrk/dot_general | solution.py:81
  112.3 3.9 bitcast_add_fusion.2
  125.3 4.8 %fusion.155 = bf16[8,384,512]{1,2,0:T(8,128)(2,1)} fusion(f32[8,384]{1,0:T(8,128)S(1)} %bitcast.393, f32[8,384]{1,0:T(8,128)S(1)} %bitcast.391, f32[8,384]{1,0:T(8,128)S(1)} %bitcast.389, f32[512,384,8]{1,0,2:T(8,128)S(1)} %fusion.154, pred[384,512]{0,1:T(8,128)(4,1)S(1)} %compare_and_fusion.2, bf16[384,1,8,128]{3,0,2,1:T(8,128)(2,1)S(1)} %copy-done.13, ...), kind=kOutput, calls=%fused_computation.8.clone.1 | convolution fusion | flops 415236096 | bytes 10588672 | tf_op jit(solution)/shard_map/while/body/eval_jaxpr/rhgd,khd->hgrk/dot_general | solution.py:81
  130.1 4.4 %bitcast_add_fusion.2 = f32[384,1,8,128]{0,3,2,1:T(8,128)} fusion(f32[384,1,8,128]{0,3,2,1:T(8,128)} %get-tuple-element.430, bf16[8,384,512]{1,2,0:T(8,128)(2,1)} %fusion.155, pred[]{:T(512)S(6)} %compare.24, bf16[4,512,1,128]{3,1,2,0:T(8,128)(2,1)S(1)} %get-tuple-element.449, s32[]{:T(128)} %get-tuple-element.429), kind=kOutput, calls=%fused_computation.12.clone.1 | convolution fusion | flops 403439616 | bytes 6422533 | tf_op jit(solution)/shard_map/while/body/eval_jaxpr/hgrk,khd->rhgd/dot_general | solution.py:132
  143.6 4.8 %fusion.155 = bf16[8,384,512]{1,2,0:T(8,128)(2,1)} fusion(f32[8,384]{1,0:T(8,128)S(1)} %bitcast.393, f32[8,384]{1,0:T(8,128)S(1)} %bitcast.391, f32[8,384]{1,0:T(8,128)S(1)} %bitcast.389, f32[512,384,8]{1,0,2:T(8,128)S(1)} %fusion.154, pred[384,512]{0,1:T(8,128)(4,1)S(1)} %compare_and_fusion.2, bf16[384,1,8,128]{3,0,2,1:T(8,128)(2,1)S(1)} %copy-done.13, ...), kind=kOutput, calls=%fused_computation.8.clone.1 | convolution fusion | flops 415236096 | bytes 10588672 | tf_op jit(solution)/shard_map/while/body/eval_jaxpr/rhgd,khd->hgrk/dot_general | solution.py:81
  148.4 4.4 %bitcast_add_fusion.2 = f32[384,1,8,128]{0,3,2,1:T(8,128)} fusion(f32[384,1,8,128]{0,3,2,1:T(8,128)} %get-tuple-element.430, bf16[8,384,512]{1,2,0:T(8,128)(2,1)} %fusion.155, pred[]{:T(512)S(6)} %compare.24, bf16[4,512,1,128]{3,1,2,0:T(8,128)(2,1)S(1)} %get-tuple-element.449, s32[]{:T(128)} %get-tuple-element.429), kind=kOutput, calls=%fused_computation.12.clone.1 | convolution fusion | flops 403439616 | bytes 6422533 | tf_op jit(solution)/shard_map/while/body/eval_jaxpr/hgrk,khd->rhgd/dot_general | solution.py:132
  162.0 4.8 %fusion.155 = bf16[8,384,512]{1,2,0:T(8,128)(2,1)} fusion(f32[8,384]{1,0:T(8,128)S(1)} %bitcast.393, f32[8,384]{1,0:T(8,128)S(1)} %bitcast.391, f32[8,384]{1,0:T(8,128)S(1)} %bitcast.389, f32[512,384,8]{1,0,2:T(8,128)S(1)} %fusion.154, pred[384,512]{0,1:T(8,128)(4,1)S(1)} %compare_and_fusion.2, bf16[384,1,8,128]{3,0,2,1:T(8,128)(2,1)S(1)} %copy-done.13, ...), kind=kOutput, calls=%fused_computation.8.clone.1 | convolution fusion | flops 415236096 | bytes 10588672 | tf_op jit(solution)/shard_map/while/body/eval_jaxpr/rhgd,khd->hgrk/dot_general | solution.py:81
  166.7 4.4 %bitcast_add_fusion.2 = f32[384,1,8,128]{0,3,2,1:T(8,128)} fusion(f32[384,1,8,128]{0,3,2,1:T(8,128)} %get-tuple-element.430, bf16[8,384,512]{1,2,0:T(8,128)(2,1)} %fusion.155, pred[]{:T(512)S(6)} %compare.24, bf16[4,512,1,128]{3,1,2,0:T(8,128)(2,1)S(1)} %get-tuple-element.449, s32[]{:T(128)} %get-tuple-element.429), kind=kOutput, calls=%fused_computation.12.clone.1 | convolution fusion | flops 403439616 | bytes 6422533 | tf_op jit(solution)/shard_map/while/body/eval_jaxpr/hgrk,khd->rhgd/dot_general | solution.py:132
  178.7 2.9 fusion.60
  183.0 13.0 %fusion.111 = f32[256,5120]{1,0:T(8,128)} fusion(bf16[256,1024]{0,1:T(8,128)(2,1)S(1)} %bitcast.385, bf16[5120,1024]{1,0:T(8,128)(2,1)} %param.25), kind=kOutput, calls=%fused_computation.152 | convolution fusion | flops 2684354560 | bytes 16252928 | tf_op jit(solution)/shard_map/rc,dc->rd/dot_general | solution.py:172
  196.0 6.3 %convolution_add_fusion.1 = f32[256,5120]{1,0:T(8,128)} fusion(f32[256,5120]{1,0:T(8,128)} %fusion.111, bf16[5120,128]{1,0:T(8,128)(2,1)S(1)} %copy-done, bf16[8,256,256]{1,2,0:T(8,128)(2,1)} %copy-done.6, bf16[256,1024]{1,0:T(8,128)(2,1)S(1)} %copy-done.8), kind=kOutput, calls=%fused_computation.52 | convolution fusion | flops 471105536 | bytes 13369344 | tf_op jit(solution)/shard_map/rc,dc->rd/dot_general | solution.py:173
  202.3 6.7 %fusion.42 = bf16[256,5120]{1,0:T(8,128)(2,1)} fusion(f32[256,5120]{1,0:T(8,128)} %convolution_add_fusion.1, bf16[5120,128]{1,0:T(8,128)(2,1)} %param.27, f32[256,256,8]{1,0,2:T(8,128)} %copy-done.5, f32[8,256]{1,0:T(8,128)S(1)} %slice_bitcast_fusion.1, f32[8,256]{1,0:T(8,128)S(1)} %slice_bitcast_fusion.2, pred[256,256]{0,1:T(8,128)(4,1)S(1)} %fusion.84, ...), kind=kOutput, calls=%fused_computation.53 | convolution fusion | flops 475037696 | bytes 11878400 | tf_op jit(solution)/shard_map/rc,dc->rd/dot_general | solution.py:174
  209.0 9.2 %fusion.110 = f32[128,5120]{1,0:T(8,128)} fusion(bf16[128,1024]{0,1:T(8,128)(2,1)S(1)} %bitcast.381, bf16[5120,1024]{1,0:T(8,128)(2,1)} %param.25), kind=kOutput, calls=%fused_computation.151 | convolution fusion | flops 1342177280 | bytes 13369344 | tf_op jit(solution)/shard_map/rc,dc->rd/dot_general | solution.py:172
  218.2 17.9 %reduce-scatter.6.cloned.1.call-done = bf16[128,1,128]{2,0,1:T(8,128)(2,1)} async-done(((bf16[2048,1,128]{2,0,1:T(8,128)(2,1)}), bf16[128,1,128]{2,0,1:T(8,128)(2,1)}) %reduce-scatter.6.cloned.1.call-update) | async-done | bytes 32784 | tf_op jit(solution)/shard_map/reduce_scatter | solution.py:178
  236.2 3.8 convolution_add_fusion.3
  239.9 57.8 %reduce-scatter.8.cloned.1.call-done = bf16[128,1,128]{2,0,1:T(8,128)(2,1)} async-done(((bf16[2048,1,128]{2,0,1:T(8,128)(2,1)}), bf16[128,1,128]{2,0,1:T(8,128)(2,1)}) %reduce-scatter.8.cloned.1.call-update) | async-done | bytes 32784 | tf_op jit(solution)/shard_map/reduce_scatter | solution.py:181
  302.4 6.3 %copy.83 = bf16[384,5120]{0,1:T(8,128)(2,1)} copy(bf16[384,5120]{1,0:T(8,128)(2,1)} %pad_maximum_fusion) | data formatting | bytes 7864320
  308.7 82.3 %reduce-scatter.10.cloned.1.call-done = bf16[640,384]{1,0:T(8,128)(2,1)} async-done(((bf16[5120,384]{1,0:T(8,128)(2,1)}), bf16[640,384]{1,0:T(8,128)(2,1)}) %reduce-scatter.10.cloned.1.call-update) | async-done | bytes 491536
  (141 shorter events, 66.7 us)
Async XLA Ops:
  7.2 188.8 %copy-start = (bf16[5120,128]{1,0:T(8,128)(2,1)S(1)}, bf16[5120,128]{1,0:T(8,128)(2,1)}, u32[]{:S(2)}) copy-start(bf16[5120,128]{1,0:T(8,128)(2,1)} %param.26) | copy-start | bytes 3932164
  7.2 28.9 %copy-start.16 = (bf16[128,1024]{1,0:T(8,128)(2,1)S(1)}, bf16[128,1024]{1,0:T(8,128)(2,1)}, u32[]{:S(2)}) copy-start(bf16[128,1024]{1,0:T(8,128)(2,1)} %param.18) | copy-start | bytes 786436
  7.2 29.7 %copy-start.22 = (bf16[128,128]{1,0:T(8,128)(2,1)S(1)}, bf16[128,128]{1,0:T(8,128)(2,1)}, u32[]{:S(2)}) copy-start(bf16[128,128]{1,0:T(8,128)(2,1)} %param.17) | copy-start | bytes 98308
  7.2 229.0 %reduce-scatter.6.cloned.1.call-start = ((), (), s32[]{:S(2)}) async-start(), calls=%async_computation.3 | async-start | bytes 557056 | tf_op jit(solution)/shard_map/reduce_scatter | solution.py:178
  73.4 11.8 %copy-start.9 = (bf16[384,1024]{0,1:T(8,128)(2,1)S(1)}, bf16[384,1024]{0,1:T(8,128)(2,1)}, u32[]{:S(2)}) copy-start(bf16[384,1024]{0,1:T(8,128)(2,1)} %pad_maximum_fusion.2) | copy-start | bytes 2359300
  73.4 11.8 %copy-start.15 = (bf16[2048,128]{1,0:T(8,128)(2,1)S(1)}, bf16[2048,128]{1,0:T(8,128)(2,1)}, u32[]{:S(2)}) copy-start(bf16[2048,128]{1,0:T(8,128)(2,1)} %all-gather.1) | copy-start | bytes 1572868
  85.2 12.9 %copy-start.7 = (bf16[256,1024]{1,0:T(8,128)(2,1)S(1)}, bf16[256,1024]{1,0:T(8,128)(2,1)}, u32[]{:S(2)}) copy-start(bf16[256,1024]{1,0:T(8,128)(2,1)} %param.19) | copy-start | bytes 1572868
  85.3 12.9 %copy-start.17 = (bf16[256,128]{1,0:T(8,128)(2,1)S(1)}, bf16[256,128]{1,0:T(8,128)(2,1)}, u32[]{:S(2)}) copy-start(bf16[256,128]{1,0:T(8,128)(2,1)} %param.20) | copy-start | bytes 196612
  85.3 14.7 %copy-start.11 = (bf16[256,1024]{1,0:T(8,128)(2,1)S(1)}, bf16[256,1024]{1,0:T(8,128)(2,1)}, u32[]{:S(2)}) copy-start(bf16[256,1024]{1,0:T(8,128)(2,1)} %param.22) | copy-start | bytes 1572868
  85.3 14.7 %copy-start.18 = (bf16[256,128]{1,0:T(8,128)(2,1)S(1)}, bf16[256,128]{1,0:T(8,128)(2,1)}, u32[]{:S(2)}) copy-start(bf16[256,128]{1,0:T(8,128)(2,1)} %param.21) | copy-start | bytes 196612
  103.8 3.6 copy-start.13
  112.3 3.9 copy-start.1
  112.3 5.6 %copy-start.3 = (f32[512,384,8]{1,0,2:T(8,128)S(1)}, f32[512,384,8]{1,0,2:T(8,128)}, u32[]{:S(2)}) copy-start(f32[512,384,8]{1,0,2:T(8,128)} %copy-done.2) | copy-start | bytes 18874372 | tf_op jit(solution)/shard_map/while
  130.1 4.4 %copy-start.1 = (bf16[8,384,512]{1,2,0:T(8,128)(2,1)S(1)}, bf16[8,384,512]{1,2,0:T(8,128)(2,1)}, u32[]{:S(2)}) copy-start(bf16[8,384,512]{1,2,0:T(8,128)(2,1)} %fusion.155) | copy-start | bytes 9437188 | tf_op jit(solution)/shard_map/while
  130.1 6.0 %copy-start.3 = (f32[512,384,8]{1,0,2:T(8,128)S(1)}, f32[512,384,8]{1,0,2:T(8,128)}, u32[]{:S(2)}) copy-start(f32[512,384,8]{1,0,2:T(8,128)} %copy-done.2) | copy-start | bytes 18874372 | tf_op jit(solution)/shard_map/while
  148.4 4.4 %copy-start.1 = (bf16[8,384,512]{1,2,0:T(8,128)(2,1)S(1)}, bf16[8,384,512]{1,2,0:T(8,128)(2,1)}, u32[]{:S(2)}) copy-start(bf16[8,384,512]{1,2,0:T(8,128)(2,1)} %fusion.155) | copy-start | bytes 9437188 | tf_op jit(solution)/shard_map/while
  148.4 6.0 %copy-start.3 = (f32[512,384,8]{1,0,2:T(8,128)S(1)}, f32[512,384,8]{1,0,2:T(8,128)}, u32[]{:S(2)}) copy-start(f32[512,384,8]{1,0,2:T(8,128)} %copy-done.2) | copy-start | bytes 18874372 | tf_op jit(solution)/shard_map/while
  166.7 4.4 %copy-start.1 = (bf16[8,384,512]{1,2,0:T(8,128)(2,1)S(1)}, bf16[8,384,512]{1,2,0:T(8,128)(2,1)}, u32[]{:S(2)}) copy-start(bf16[8,384,512]{1,2,0:T(8,128)(2,1)} %fusion.155) | copy-start | bytes 9437188 | tf_op jit(solution)/shard_map/while
  166.7 6.0 %copy-start.3 = (f32[512,384,8]{1,0,2:T(8,128)S(1)}, f32[512,384,8]{1,0,2:T(8,128)}, u32[]{:S(2)}) copy-start(f32[512,384,8]{1,0,2:T(8,128)} %copy-done.2) | copy-start | bytes 18874372 | tf_op jit(solution)/shard_map/while
  175.8 6.8 %copy-start.4 = (f32[384,1,8,128]{0,3,2,1:T(8,128)S(1)}, f32[384,1,8,128]{0,3,2,1:T(8,128)}, u32[]{:S(2)}) copy-start(f32[384,1,8,128]{0,3,2,1:T(8,128)} %get-tuple-element.178) | copy-start | bytes 4718596
  175.8 122.0 %reduce-scatter.8.cloned.1.call-start = ((), (), s32[]{:S(2)}) async-start(), calls=%async_computation.4 | async-start | bytes 557056 | tf_op jit(solution)/shard_map/reduce_scatter | solution.py:181
  176.5 214.5 %reduce-scatter.10.cloned.1.call-start = ((), (), s32[]{:S(2)}) async-start(), calls=%async_computation.5 | async-start | bytes 4423680
  183.0 13.0 %copy-start.8 = (bf16[256,1024]{1,0:T(8,128)(2,1)S(1)}, bf16[256,1024]{1,0:T(8,128)(2,1)}, u32[]{:S(2)}) copy-start(bf16[256,1024]{1,0:T(8,128)(2,1)} %param.19) | copy-start | bytes 1572868
  218.2 79.5 %copy-start.12 = (bf16[5120,128]{1,0:T(8,128)(2,1)S(1)}, bf16[5120,128]{1,0:T(8,128)(2,1)}, u32[]{:S(2)}) copy-start(bf16[5120,128]{1,0:T(8,128)(2,1)} %param.27) | copy-start | bytes 3932164
  (17 other events, 35.0 us)
Sparse Core Ops, SparseCore 0:
  175.9 60.1 reduce-scatter.5
  238.6 59.0 reduce-scatter.7
  308.9 82.1 reduce-scatter.9
where the time goes:
time: 402 us; the launch traced here: 401 us
  waiting for transfers between devices  159 us (40%)
  matrix products  124 us (31%)
  blocking collectives  42.4 us (11%)
  local copies, waits for them, and re-layouts  36.2 us (9%)
  other arithmetic  25.4 us (6%)
  between operations  14 us (3%)
    unnamed x4, waiting for transfers between devices  83 us
    reduce_scatter x1, waiting for transfers between devices, shards(): lax.psum_scatter(dvalue_whole.astype(jnp.bfloat16), 'seq', scatter_dimens...  57.8 us
    dot_general x5, matrix products, scores_of(): jnp.einsum('rhgd,khd->hgrk', do_all, values, preferred_element_type=jnp.f...  32 us
    all_gather x1, blocking collectives, shards(): lax.all_gather(keys_mine, 'seq', axis=0, tiled=True)  22.5 us
    dot_general x2, matrix products, input_term(): jnp.einsum('rc,dc->rd', dquery, w_query, preferred_element_type=jnp.float32)  22.2 us
    all_gather x1, blocking collectives, shards(): lax.all_gather(values_mine, 'seq', axis=0, tiled=True)  20 us
    unnamed x45, local copies, waits for them, and re-layouts  19 us
    reduce_scatter x1, waiting for transfers between devices, shards(): lax.psum_scatter(dkey_whole.astype(jnp.bfloat16), 'seq', scatter_dimensio...  17.9 us
  transfers between devices with their start and end apart: 3, of which 3 were waited for; matrix products, arithmetic and copies ran while one was open for 11% of the time, Pallas kernels for 0%

commit v1 on v0

v1 whole, which is shorter than its diff:
```python
import functools
import math

import jax
import jax.numpy as jnp
from jax import lax
from jax.experimental import pallas as pl
from jax.experimental.pallas import tpu as pltpu
from jax.sharding import PartitionSpec as P

MESH = pl.DeviceIdType.MESH
VMEM = pltpu.VMEM
BF16 = jnp.bfloat16
F32 = jnp.float32
HD = 128
GROUP = 8
TOK = 128
NEG = -1e30
SCALE = 1.0 / math.sqrt(HD)
EXP2 = SCALE * math.log2(math.e)
D = 5120
COLS = 640
WIDE = 1280
NT = (((1,), (1,)), ((), ()))
NN = (((1,), (0,)), ((), ()))


def dot(a, b, dims):
    return lax.dot_general(a, b, dims, preferred_element_type=F32)


def remote(src, dst, send, recv, seq, head):
    return pltpu.make_async_remote_copy(
        src_ref=src, dst_ref=dst, send_sem=send, recv_sem=recv,
        device_id=(seq, head), device_id_type=MESH,
    )


def seq_place():
    n = lax.axis_index("seq")
    return n // 4, lax.rem(n // 2, 2), lax.rem(n, 2)


def seq_peer(dy, dx):
    y, x, c = seq_place()
    return lax.rem(y + dy + 4, 4) * 4 + lax.rem(x + dx, 2) * 2 + c


def seq_sibling():
    n = lax.axis_index("seq")
    return n + 1 - 2 * lax.rem(n, 2)


SEQ_STEPS = [(0, 1), (1, 0), (3, 0), (1, 1), (3, 1), (2, 0), (2, 1)]


def head_peers():
    h = lax.axis_index("head")
    x, z = h // 4, lax.rem(h, 4)
    base = x * 4
    z1 = base + z + 1 - 2 * lax.rem(z, 2)
    z3 = base + 3 - z
    flip = (1 - x) * 4 + z
    return z1, z3, flip


def gather_copies(kv, send, recv, fsend, frecv):
    n, head = lax.axis_index("seq"), lax.axis_index("head")
    sib = seq_sibling()
    firsts = [remote(kv.at[n], kv.at[n], fsend.at[0], frecv.at[0], sib, head)]
    for j, (dy, dx) in enumerate(SEQ_STEPS):
        firsts.append(
            remote(kv.at[n], kv.at[n], send.at[j], recv.at[j], seq_peer(dy, dx), head)
        )
    return firsts


def gather_start(kv, send, recv, fsend, frecv):
    for copy in gather_copies(kv, send, recv, fsend, frecv):
        copy.start()


def gather_finish(kv, send, recv, fsend, frecv):
    head = lax.axis_index("head")
    sib = seq_sibling()
    firsts = gather_copies(kv, send, recv, fsend, frecv)
    forwards = []
    for j, (dy, dx) in enumerate(SEQ_STEPS):
        src = seq_peer(-dy, dx)
        firsts[j + 1].wait_recv()
        forward = remote(kv.at[src], kv.at[src], fsend.at[j + 1], frecv.at[j + 1], sib, head)
        forward.start()
        forwards.append(forward)
    for copy in [firsts[0]] + forwards:
        copy.wait_recv()
    for copy in firsts + forwards:
        copy.wait_send()


def gather_kernel(k_ref, v_ref, kv, send, recv, fsend, frecv):
    n, head = lax.axis_index("seq"), lax.axis_index("head")
    kv[n, 0] = k_ref[...]
    kv[n, 1] = v_ref[...]
    barrier = pltpu.get_barrier_semaphore()
    peers = [seq_sibling()] + [seq_peer(dy, dx) for dy, dx in SEQ_STEPS]
    for peer in peers:
        pl.semaphore_signal(barrier, inc=1, device_id=(peer, head), device_id_type=MESH)
    pl.semaphore_wait(barrier, len(peers))
    gather_start(kv, send, recv, fsend, frecv)
    gather_finish(kv, send, recv, fsend, frecv)


def gather(k, v):
    return pl.pallas_call(
        gather_kernel,
        out_shape=jax.ShapeDtypeStruct((16, 2, TOK, HD), BF16),
        in_specs=[pl.BlockSpec(memory_space=VMEM)] * 2,
        out_specs=pl.BlockSpec(memory_space=VMEM),
        scratch_shapes=[
            pltpu.SemaphoreType.DMA((7,)),
            pltpu.SemaphoreType.DMA((7,)),
            pltpu.SemaphoreType.DMA((8,)),
            pltpu.SemaphoreType.DMA((8,)),
        ],
        compiler_params=pltpu.CompilerParams(
            collective_id=0, has_side_effects=True, vmem_limit_bytes=32 << 20
        ),
        name="gather_kv",
    )(k, v)


def segment_of(place, lens_ref):
    end = jnp.int32(0)
    seg = jnp.zeros(place.shape, jnp.int32)
    for c in range(4):
        end = end + lens_ref[0, c]
        seg = seg + (place >= end).astype(jnp.int32)
    return seg


def prompt_of(seg, prompt_ref):
    out = jnp.zeros(seg.shape, jnp.int32)
    for c in range(4):
        out = jnp.where(seg == c, prompt_ref[0, c], out)
    return out


def load_keys(kv, k_r, v_r, kke, vve, kket):
    for r in range(8):
        rows = pl.ds(r * TOK, TOK)
        kke[rows, :HD] = kv[r, 0]
        kke[rows, HD:] = kv[8 + r, 0]
        vve[rows, :HD] = kv[r, 1]
        vve[rows, HD:] = kv[8 + r, 1]
    local = pl.ds(1024, 256)
    kke[local, :HD] = k_r[...]
    kke[local, HD:] = k_r[...]
    vve[local, :HD] = v_r[...]
    vve[local, HD:] = v_r[...]
    for r in range(10):
        rows = pl.ds(r * TOK, TOK)
        kket[:, rows] = kke[rows, :].T


def load_rows(q, do, col_prompt, qext, doext):
    first = col_prompt == 0
    zero = jnp.zeros((TOK, HD), BF16)
    first = jnp.broadcast_to(first, (TOK, HD))
    for h in range(GROUP):
        lanes = pl.ds(h * HD, HD)
        rows = pl.ds(h * TOK, TOK)
        qv, dov = q[:, lanes], do[:, lanes]
        qext[rows, :HD] = jnp.where(first, qv, zero)
        qext[rows, HD:] = jnp.where(first, zero, qv)
        doext[rows, :HD] = jnp.where(first, dov, zero)
        doext[rows, HD:] = jnp.where(first, zero, dov)


def fold(x, op):
    return op(x.reshape(TOK // 8, 8, x.shape[1]), axis=0)


def head_pair(hp, tiles, bias_of, qext, doext, kke, vve, s_ref, dp_ref, et, dst):
    rows = pl.ds(pl.multiple_of(hp * 256, 256), 256)
    qe, doe = qext[rows, :], doext[rows, :]
    top = jnp.full((8, 256), NEG, F32)
    for t in range(tiles):
        keys = pl.ds(t * TOK, TOK)
        s = dot(kke[keys, :], qe, NT)
        s = bias_of(t, s)
        s_ref[keys, :] = s
        top = jnp.maximum(top, fold(s, jnp.max))
        dp_ref[keys, :] = dot(vve[keys, :], doe, NT)
    top = jnp.max(top, axis=0, keepdims=True)
    norm = jnp.zeros((8, 256), F32)
    weighted = jnp.zeros((8, 256), F32)
    for t in range(tiles):
        keys = pl.ds(t * TOK, TOK)
        e = jnp.exp2((s_ref[keys, :] - top) * EXP2)
        s_ref[keys, :] = e
        norm = norm + fold(e, jnp.sum)
        weighted = weighted + fold(e * dp_ref[keys, :], jnp.sum)
    inv = 1.0 / jnp.sum(norm, axis=0, keepdims=True)
    mean = jnp.sum(weighted, axis=0, keepdims=True) * inv
    for t in range(tiles):
        keys = pl.ds(t * TOK, TOK)
        p = s_ref[keys, :] * inv
        et[keys, rows] = p.astype(BF16)
        dst[keys, rows] = (p * (dp_ref[keys, :] - mean)).astype(BF16)


def chunk_products(tiles, first, qext, doext, kket, et, dst, dkk, dvv):
    for t in range(tiles):
        keys = pl.ds(t * TOK, TOK)
        dv = dot(et[keys, :], doext[...], NN)
        dk = dot(dst[keys, :], qext[...], NN)
        if first:
            dvv[keys, :] = dv
            dkk[keys, :] = dk
        else:
            dvv[keys, :] += dv
            dkk[keys, :] += dk


def chunk_dq(tiles, row_prompt, kket, dst, dq_ref, rows_out):
    keys = pl.ds(0, tiles * TOK)
    first = row_prompt == 0
    for hp in range(4):
        rows = pl.ds(hp * 256, 256)
        both = dot(kket[:, keys], dst[keys, rows], NN)
        for k in range(2):
            lanes = slice(k * TOK, (k + 1) * TOK)
            part = jnp.where(first, both[:HD, lanes], both[HD:, lanes]) * SCALE
            h = hp * 2 + k
            dq_ref[rows_out, h * HD : (h + 1) * HD] = part.T.astype(BF16)


def attention_kernel(
    lens_ref, prompt_ref, kv, q_p, do_p, q_r, do_r, k_r, v_r,
    d_r, dq_p, grads,
    kke, vve, kket, qext, doext, s_ref, dp_ref, et, dst, dkk, dvv, bias,
):
    n = lax.axis_index("seq")
    load_keys(kv, k_r, v_r, kke, vve, kket)

    for number, half in enumerate((1, 0)):
        tiles = 8 + half + 1
        count = (half + 1) * TOK
        base = half * TOK
        col = base + lax.broadcasted_iota(jnp.int32, (TOK, 1), 0)
        col_prompt = prompt_of(segment_of(col, lens_ref), prompt_ref)
        row = base + lax.rem(lax.broadcasted_iota(jnp.int32, (1, 256), 1), TOK)
        row_seg = segment_of(row, lens_ref)
        row_prompt = prompt_of(row_seg[:, :TOK], prompt_ref)
        key = lax.broadcasted_iota(jnp.int32, (count, 1), 0)
        key_seg = segment_of(key, lens_ref)
        seen = (key_seg == row_seg) & (key <= row)
        bias[:count, :] = jnp.where(seen, 0.0, NEG)
        span = slice(base, base + TOK)
        load_rows(q_r.at[span], do_r.at[span], col_prompt, qext, doext)

        def local_bias(t, s):
            if t < 8:
                return s
            return s + bias[(t - 8) * TOK : (t - 7) * TOK, :]

        def visit(hp, c):
            head_pair(
                hp, tiles, local_bias, qext, doext, kke, vve, s_ref, dp_ref, et, dst
            )
            return c

        lax.fori_loop(0, 4, visit, 0)
        if number == 0:
            chunk_products(tiles, True, qext, doext, kket, et, dst, dkk, dvv)
        else:
            chunk_products(tiles, False, qext, doext, kket, et, dst, dkk, dvv)
        chunk_dq(tiles, row_prompt, kket, dst, d_r, span)

    place = lax.rem(n, 8) * TOK
    diff = (
        place
        + lax.rem(lax.broadcasted_iota(jnp.int32, (TOK, 256), 1), TOK)
        - lax.broadcasted_iota(jnp.int32, (TOK, 256), 0)
    )
    mine = n // 8
    load_rows(q_p, do_p, jnp.full((TOK, 1), mine, jnp.int32), qext, doext)

    def causal(t, s):
        return jnp.where(diff >= t * TOK, s, NEG)

    def visit(hp, c):
        head_pair(hp, 8, causal, qext, doext, kke, vve, s_ref, dp_ref, et, dst)
        return c

    lax.fori_loop(0, 4, visit, 0)
    chunk_products(8, False, qext, doext, kket, et, dst, dkk, dvv)
    chunk_dq(8, jnp.full((1, TOK), mine, jnp.int32), kket, dst, dq_p, slice(0, TOK))

    local = slice(1024, WIDE)
    d_r[:, 1024:1152] = ((dkk[local, :HD] + dkk[local, HD:]) * SCALE).astype(BF16)
    d_r[:, 1152:] = (dvv[local, :HD] + dvv[local, HD:]).astype(BF16)
    for r in range(8):
        keys = slice(r * TOK, (r + 1) * TOK)
        for p in range(2):
            lanes = slice(p * HD, (p + 1) * HD)
            grads[r, p, :, :HD] = (dkk[keys, lanes] * SCALE).astype(BF16)
            grads[r, p, :, HD:] = dvv[keys, lanes].astype(BF16)


def attention(lens, prompts, kv, q_p, do_p, q_r, do_r, k_r, v_r):
    whole = pl.BlockSpec(memory_space=VMEM)
    scalars = pl.BlockSpec(memory_space=pltpu.SMEM)
    return pl.pallas_call(
        attention_kernel,
        out_shape=(
            jax.ShapeDtypeStruct((256, WIDE), BF16),
            jax.ShapeDtypeStruct((TOK, 1024), BF16),
            jax.ShapeDtypeStruct((8, 2, TOK, 256), BF16),
        ),
        in_specs=[scalars] * 2 + [whole] * 7,
        out_specs=(whole,) * 3,
        scratch_shapes=[
            VMEM((WIDE, 256), BF16),
            VMEM((WIDE, 256), BF16),
            VMEM((256, WIDE), BF16),
            VMEM((1024, 256), BF16),
            VMEM((1024, 256), BF16),
            VMEM((WIDE, 256), F32),
            VMEM((WIDE, 256), F32),
            VMEM((WIDE, 1024), BF16),
            VMEM((WIDE, 1024), BF16),
            VMEM((WIDE, 256), F32),
            VMEM((WIDE, 256), F32),
            VMEM((256, 256), F32),
        ],
        compiler_params=pltpu.CompilerParams(vmem_limit_bytes=48 << 20),
        name="attention",
    )(lens, prompts, kv, q_p, do_p, q_r, do_r, k_r, v_r)


SIDES = (
    dict(give=(1, 3), keep=(0, 3), last=1),
    dict(give=(2, 4), keep=(1, 0), last=0),
)


def owner_of(offset, side):
    h = lax.axis_index("head")
    x, z = h // 4, lax.rem(h, 4)
    if offset == 0:
        oz = z
    elif offset == 1:
        oz = z + 1 - 2 * lax.rem(z, 2)
    elif offset == 2:
        oz = lax.rem(z + 2, 4)
    else:
        oz = 3 - z
    ox = x if side == 0 else 1 - x
    return ox * 4 + oz


WEIGHT_ORDER = (2, 1, 3, 0)


def weight_copies(offsets, w_q, w_k, w_v, w, sem):
    for offset in offsets:
        for side in range(2):
            rows = pl.ds(pl.multiple_of(owner_of(offset, side) * COLS, COLS), COLS)
            into = pl.ds(side * COLS, COLS)
            yield from [
                pltpu.make_async_copy(w_q.at[rows], w.at[offset, into, pl.ds(0, 1024)], sem.at[offset, side, 0]),
                pltpu.make_async_copy(w_k.at[rows], w.at[offset, into, pl.ds(1024, HD)], sem.at[offset, side, 1]),
                pltpu.make_async_copy(w_v.at[rows], w.at[offset, into, pl.ds(1152, HD)], sem.at[offset, side, 2]),
            ]


class HeadSum:
    def __init__(self, chunk, terms, r1, s2, r2, s3, r3, sems):
        self.chunk = chunk
        self.terms, self.r1, self.s2, self.r2, self.s3, self.r3 = (
            terms.at[chunk], r1.at[chunk], s2.at[chunk], r2.at[chunk], s3.at[chunk], r3.at[chunk]
        )
        self.sems = sems
        self.seq = lax.axis_index("seq")
        self.z1, self.z3, self.flip = head_peers()

    def copy(self, half, step):
        send, recv = (self.sems.at[k, self.chunk, half, step] for k in range(2))
        near, far = (self.z1, self.z3) if half == 0 else (self.z3, self.z1)
        if step == 0:
            low, high = SIDES[half]["give"]
            src = self.terms.at[pl.ds(low, high - low), :, pl.ds(half * 64, 64), :]
            return remote(src, self.r1.at[half], send, recv, self.seq, near)
        if step == 1:
            return remote(self.s2.at[half], self.r2.at[half], send, recv, self.seq, self.flip)
        return remote(self.s3.at[half], self.r3.at[half], send, recv, self.seq, far)

    def first(self, half):
        self.copy(half, 0).start()

    def second(self, half):
        self.copy(half, 0).wait_recv()
        rows = slice(half * 64, half * 64 + 64)
        for k, offset in enumerate(SIDES[half]["keep"]):
            total = self.terms[offset, 1, rows, :].astype(F32) + self.r1[half, k, 1].astype(F32)
            self.s2[half, k] = total.astype(BF16)
        self.copy(half, 1).start()

    def kept(self, half, k):
        rows = slice(half * 64, half * 64 + 64)
        offset = SIDES[half]["keep"][k]
        return (
            self.terms[offset, 0, rows, :].astype(F32)
            + self.r1[half, k, 0].astype(F32)
            + self.r2[half, k].astype(F32)
        )

    def third(self, half):
        self.copy(half, 1).wait_recv()
        self.s3[half] = self.kept(half, SIDES[half]["last"]).astype(BF16)
        self.copy(half, 2).start()

    def final(self, half, out, base):
        total = self.kept(half, 1 - SIDES[half]["last"])
        self.copy(half, 2).wait_recv()
        out[base + half * 64 : base + half * 64 + 64, :] = (
            total + self.r3[half].astype(F32)
        ).astype(BF16)

    def drain(self):
        for half in range(2):
            for step in range(3):
                self.copy(half, step).wait_send()


def project(d, w, terms, chunk, wait_weights):
    rows = d[...]
    for offset in WEIGHT_ORDER:
        wait_weights(offset)
        for part in range(5):
            block = dot(rows, w[offset, part * 256 : (part + 1) * 256, :], NT).astype(BF16)
            for piece in range(2):
                col = part * 256 + piece * 128
                side, lane = divmod(col, COLS)
                terms[chunk, offset, side, :, lane : lane + 128] = block[:, piece * 128 : piece * 128 + 128]


def grads_sibling(grads, rc, gsem):
    c = lax.rem(lax.axis_index("seq"), 2)
    return remote(
        grads.at[:, 1 - c], rc, gsem.at[0, 7], gsem.at[1, 7], seq_sibling(), lax.axis_index("head")
    )


def grads_copies(gs, rg, gsem):
    y, x, c = seq_place()
    copies = []
    for j, (dy, dx) in enumerate(SEQ_STEPS):
        oy = lax.rem(y + dy, 4)
        ox = lax.rem(x + dx, 2)
        block = lax.rem(oy, 2) * 2 + ox
        copies.append(
            remote(
                gs.at[block, oy // 2], rg.at[j], gsem.at[0, j], gsem.at[1, j],
                seq_peer(dy, dx), lax.axis_index("head"),
            )
        )
    return copies


def grads_second(grads, rc, gs, rg, gsem):
    c = lax.rem(lax.axis_index("seq"), 2)
    grads_sibling(grads, rc, gsem).wait_recv()
    for b in range(4):
        for p in range(2):
            gs[b, p] = (grads[b, c, p].astype(F32) + rc[b, p].astype(F32)).astype(BF16)
    for copy in grads_copies(gs, rg, gsem):
        copy.start()


def grads_finish(gs, rg, gsem, d_p):
    y, x, c = seq_place()
    total = gs[lax.rem(y, 2) * 2 + x, y // 2].astype(F32)
    for j, copy in enumerate(grads_copies(gs, rg, gsem)):
        copy.wait_recv()
        total = total + rg[j].astype(F32)
    d_p[:, 1024:] = total.astype(BF16)


def project_kernel(
    d_r, dq_p, grads, w_q, w_k, w_v,
    out_p, out_r,
    w, d_p, terms, r1, s2, r2, s3, r3, rc, gs, rg, wsem, hsem, gsem,
):
    seq, head = lax.axis_index("seq"), lax.axis_index("head")
    for copy in weight_copies(WEIGHT_ORDER, w_q, w_k, w_v, w, wsem):
        copy.start()
    barrier = pltpu.get_barrier_semaphore()
    seqs = [seq_sibling()] + [seq_peer(dy, dx) for dy, dx in SEQ_STEPS]
    heads = list(head_peers())
    for peer in seqs:
        pl.semaphore_signal(barrier, inc=1, device_id=(peer, head), device_id_type=MESH)
    for peer in heads:
        pl.semaphore_signal(barrier, inc=1, device_id=(seq, peer), device_id_type=MESH)
    pl.semaphore_wait(barrier, len(seqs) + len(heads))

    grads_sibling(grads, rc, gsem).start()
    d_p[:, :1024] = dq_p[...]

    def wait_weights(offset):
        for copy in weight_copies((offset,), w_q, w_k, w_v, w, wsem):
            copy.wait()

    sums = [HeadSum(c, terms, r1, s2, r2, s3, r3, hsem) for c in range(3)]
    project(d_r.at[0:TOK], w, terms, 0, wait_weights)
    for half in range(2):
        sums[0].first(half)
    grads_second(grads, rc, gs, rg, gsem)
    project(d_r.at[TOK:256], w, terms, 1, lambda offset: None)
    for half in range(2):
        sums[1].first(half)
    grads_finish(gs, rg, gsem, d_p)
    project(d_p, w, terms, 2, lambda offset: None)
    for half in range(2):
        sums[2].first(half)
    for c in range(3):
        for half in range(2):
            sums[c].second(half)
    for c in range(3):
        for half in range(2):
            sums[c].third(half)
    for c in range(3):
        out, base = (out_p, 0) if c == 2 else (out_r, c * TOK)
        for half in range(2):
            sums[c].final(half, out, base)
    grads_sibling(grads, rc, gsem).wait_send()
    for copy in grads_copies(gs, rg, gsem):
        copy.wait_send()
    for c in range(3):
        sums[c].drain()


def projection(d_r, dq_p, grads, w_q, w_k, w_v):
    whole = pl.BlockSpec(memory_space=VMEM)
    hbm = pl.BlockSpec(memory_space=pl.ANY)
    return pl.pallas_call(
        project_kernel,
        out_shape=(
            jax.ShapeDtypeStruct((TOK, COLS), BF16),
            jax.ShapeDtypeStruct((256, COLS), BF16),
        ),
        in_specs=[whole] * 3 + [hbm] * 3,
        out_specs=(whole,) * 2,
        scratch_shapes=[
            VMEM((4, WIDE, WIDE), BF16),
            VMEM((TOK, WIDE), BF16),
            VMEM((3, 4, 2, TOK, COLS), BF16),
            VMEM((3, 2, 2, 2, 64, COLS), BF16),
            VMEM((3, 2, 2, 64, COLS), BF16),
            VMEM((3, 2, 2, 64, COLS), BF16),
            VMEM((3, 2, 64, COLS), BF16),
            VMEM((3, 2, 64, COLS), BF16),
            VMEM((4, 2, TOK, 256), BF16),
            VMEM((4, 2, TOK, 256), BF16),
            VMEM((7, TOK, 256), BF16),
            pltpu.SemaphoreType.DMA((4, 2, 3)),
            pltpu.SemaphoreType.DMA((2, 3, 2, 3)),
            pltpu.SemaphoreType.DMA((2, 8)),
        ],
        compiler_params=pltpu.CompilerParams(
            collective_id=1, has_side_effects=True, vmem_limit_bytes=56 << 20
        ),
        name="project_sum",
    )(d_r, dq_p, grads, w_q, w_k, w_v)


def shards(
    q_prompt, k_prompt, v_prompt, do_prompt, q_resp, k_resp, v_resp, do_resp,
    resp_lengths, resp_prompt, w_query, w_key, w_value,
):
    kv = gather(k_prompt, v_prompt)
    d_r, dq_p, grads = attention(
        resp_lengths, resp_prompt, kv, q_prompt, do_prompt, q_resp, do_resp, k_resp, v_resp
    )
    grads = grads.reshape(4, 2, 2, TOK, 256)
    return projection(d_r, dq_p, grads, w_query, w_key, w_value)


def solution(mesh):
    return jax.shard_map(
        shards,
        mesh=mesh,
        in_specs=(P("seq", "head"),) * 8 + (P("seq", None),) * 2 + (P(None, "head"),) * 3,
        out_specs=(P("seq", "head"), P("seq", "head")),
        check_vma=False,
    )
```

time: 402 us -> 106 us (0.26)
  waiting for transfers between devices: 159 us -> 0 us
  matrix products: 124 us -> 0 us
  Pallas kernels: 0 us -> 92.4 us
  blocking collectives: 42.4 us -> 0 us
  other arithmetic: 25.4 us -> 0 us
  local copies, waits for them, and re-layouts: 36.2 us -> 12.3 us
  between operations: 14 us -> 0.72 us
    dot_general x31 -> x0, matrix products: 124 us -> none  [the longest x5 32 us: scores_of(): jnp.einsum('rhgd,khd->hgrk', do_all, values, preferred_element_type=jnp.f...]
    pallas_call x0 -> x3, Pallas kernels: none -> 92.4 us  [the longest x1 53.4 us: projection(): pl.pallas_call(project_kernel, out_shape=(jax.ShapeDtypeStruct((TOK, COLS...]
    unnamed x4 -> x0, waiting for transfers between devices: 83 us -> none
    reduce_scatter x2 -> x0, waiting for transfers between devices: 75.7 us -> none  [the longest x1 57.8 us: shards(): lax.psum_scatter(dvalue_whole.astype(jnp.bfloat16), 'seq', scatter_dimens...]
    all_gather x2 -> x0, blocking collectives: 42.4 us -> none  [the longest x1 22.5 us: shards(): lax.all_gather(keys_mine, 'seq', axis=0, tiled=True)]
    reduce_sum x3 -> x0, other arithmetic: 12.6 us -> none  [the longest x1 11.8 us: piece_stats(): return (top, jnp.sum(weight, axis=-1), jnp.sum(weight * grads, axis=-1))]
    while x40 -> x0, local copies, waits for them, and re-layouts: 10.8 us -> none
    unnamed x45 -> x28, local copies, waits for them, and re-layouts: 19 us -> 12.3 us
  transfers between devices with their start and end apart: 3 -> 0, of which waited for: 3 -> 0; matrix products, arithmetic and copies ran while one was open for 11% -> 0% of each run, Pallas kernels for 0% -> 0%
where the time goes in v1:
time: 106 us; the launch traced here: 105 us
  Pallas kernels  92.4 us (87%)
  local copies, waits for them, and re-layouts  12.3 us (12%)
    pallas_call x1, Pallas kernels, projection(): pl.pallas_call(project_kernel, out_shape=(jax.ShapeDtypeStruct((TOK, COLS...  53.4 us
    pallas_call x1, Pallas kernels, attention(): pl.pallas_call(attention_kernel, out_shape=(jax.ShapeDtypeStruct((256, WI...  26.3 us
    pallas_call x1, Pallas kernels, gather(): pl.pallas_call(gather_kernel, out_shape=jax.ShapeDtypeStruct((16, 2, TOK,...  12.7 us
    unnamed x28, local copies, waits for them, and re-layouts  12.3 us

profile of v1, /device:TPU:0, one launch (start us, length us, event | category | flops | bytes accessed | tf_op | source)
XLA Modules:
  0.0 105.5 jit_solution(13661846163653032322)
XLA Ops:
  0.6 0.0 copy-start.3
  0.6 0.0 copy-start.2
  0.7 0.0 copy-start.9
  0.7 0.8 copy-done.9
  1.5 0.0 copy-start.10
  1.5 0.8 copy-done.10
  2.3 12.7 %gather_kv.1.kv = bf16[16,2,128,128]{3,2,1,0:T(8,128)(2,1)S(1)} custom-call(bf16[128,128]{1,0:T(8,128)(2,1)S(1)} %copy-done.9, bf16[128,128]{1,0:T(8,128)(2,1)S(1)} %copy-done.10), custom_call_target="tpu_custom_call" | custom-call | tf_op jit(solution)/shard_map/gather_kv/pallas_call | solution.py:114
  15.0 0.0 copy-done.3
  15.0 0.0 copy-done.2
  15.0 0.0 copy-start.5
  15.0 0.9 copy-done.5
  16.0 0.9 copy-done.6
  16.9 0.8 copy-done.7
  17.7 0.8 copy-done.8
  18.6 0.7 copy-done.11
  19.2 0.7 copy-done.12
  19.9 26.3 %attention.1 = (bf16[256,1280]{1,0:T(8,128)(2,1)S(1)}, bf16[128,1024]{1,0:T(8,128)(2,1)S(1)}, bf16[8,2,128,256]{3,2,1,0:T(8,128)(2,1)S(1)}) custom-call(s32[1,4]{1,0:T(1,128)S(1)} %copy-done.11, s32[1,4]{1,0:T(1,128)S(1)} %copy-done.12, bf16[16,2,128,128]{3,2,1,0:T(8,128)(2,1)S(1)} %gather_kv.1.kv, bf16[128,1024]{1,0:T(8,128)(2,1)S(1)} %copy-done.5, ...), custom_call_target="tpu_custom_call" | custom-call | tf_op jit(solution)/shard_map/attention/pallas_call | solution.py:314
  46.2 0.0 copy-start
  46.2 1.0 copy-done
  47.2 0.9 copy-done.1
  48.1 0.7 copy-done.4
  48.8 53.4 %project_sum.1 = (bf16[128,640]{1,0:T(8,128)(2,1)}, bf16[256,640]{1,0:T(8,128)(2,1)}) custom-call(bf16[256,1280]{1,0:T(8,128)(2,1)} %copy-done.1, bf16[128,1024]{1,0:T(8,128)(2,1)} %copy-done.4, bf16[4,2,2,128,256]{4,3,2,1,0:T(8,128)(2,1)} %bitcast.1, bf16[5120,1024]{1,0:T(8,128)(2,1)} %w_q.1, bf16[5120,128]{1,0:T(8,128)(2,1)} %w_k.1, bf16[5120,128]{1,0:T(8,128)(2,1)} %w_v.1), custom_call_target="tpu_custom_call" | custom-call | tf_op jit(solution)/shard_map/project_sum/pallas_call | solution.py:547
  102.1 1.6 %copy.17 = bf16[128,640]{1,0:T(8,128)(2,1)} copy(bf16[128,640]{1,0:T(8,128)(2,1)} %get-tuple-element.10) | data formatting | bytes 327680
  103.7 1.7 %copy.18 = bf16[256,640]{1,0:T(8,128)(2,1)} copy(bf16[256,640]{1,0:T(8,128)(2,1)} %get-tuple-element.11) | data formatting | bytes 655360
  (7 shorter events, 0.0 us)
Async XLA Ops:
  0.6 14.4 %copy-start.3 = (bf16[256,1024]{1,0:T(8,128)(2,1)S(1)}, bf16[256,1024]{1,0:T(8,128)(2,1)}, u32[]{:S(2)}) copy-start(bf16[256,1024]{1,0:T(8,128)(2,1)} %do_r.1) | copy-start | bytes 1572868
  0.6 14.4 %copy-start.2 = (bf16[256,1024]{1,0:T(8,128)(2,1)S(1)}, bf16[256,1024]{1,0:T(8,128)(2,1)}, u32[]{:S(2)}) copy-start(bf16[256,1024]{1,0:T(8,128)(2,1)} %q_r.1) | copy-start | bytes 1572868
  0.7 0.8 copy-start.9
  1.5 0.8 copy-start.10
  15.0 1.0 copy-start.5
  16.0 0.9 copy-start.6
  16.9 0.8 copy-start.7
  17.7 0.8 copy-start.8
  18.6 0.7 copy-start.11
  19.2 0.7 copy-start.12
  46.2 1.0 copy-start
  47.2 0.9 copy-start.1
  48.1 0.7 copy-start.4

commit v2 on v1

v2 whole, which is shorter than its diff:
```python
import functools
import math

import jax
import jax.numpy as jnp
from jax import lax
from jax.experimental import pallas as pl
from jax.experimental.pallas import tpu as pltpu
from jax.sharding import PartitionSpec as P

MESH = pl.DeviceIdType.MESH
VMEM = pltpu.VMEM
BF16 = jnp.bfloat16
F32 = jnp.float32
HD = 128
GROUP = 8
TOK = 128
NEG = -1e30
SCALE = 1.0 / math.sqrt(HD)
EXP2 = SCALE * math.log2(math.e)
D = 5120
COLS = 640
WIDE = 1280
NT = (((1,), (1,)), ((), ()))
NN = (((1,), (0,)), ((), ()))


def dot(a, b, dims):
    return lax.dot_general(a, b, dims, preferred_element_type=F32)


def remote(src, dst, send, recv, seq, head):
    return pltpu.make_async_remote_copy(
        src_ref=src, dst_ref=dst, send_sem=send, recv_sem=recv,
        device_id=(seq, head), device_id_type=MESH,
    )


def seq_place():
    n = lax.axis_index("seq")
    return n // 4, lax.rem(n // 2, 2), lax.rem(n, 2)


def seq_peer(dy, dx):
    y, x, c = seq_place()
    return lax.rem(y + dy + 4, 4) * 4 + lax.rem(x + dx, 2) * 2 + c


def seq_sibling():
    n = lax.axis_index("seq")
    return n + 1 - 2 * lax.rem(n, 2)


SEQ_STEPS = [(0, 1), (1, 0), (3, 0), (1, 1), (3, 1), (2, 0), (2, 1)]


def head_peers():
    h = lax.axis_index("head")
    x, z = h // 4, lax.rem(h, 4)
    base = x * 4
    z1 = base + z + 1 - 2 * lax.rem(z, 2)
    z3 = base + 3 - z
    flip = (1 - x) * 4 + z
    return z1, z3, flip


def gather_copies(kv, send, recv, fsend, frecv):
    n, head = lax.axis_index("seq"), lax.axis_index("head")
    sib = seq_sibling()
    firsts = [remote(kv.at[n], kv.at[n], fsend.at[0], frecv.at[0], sib, head)]
    for j, (dy, dx) in enumerate(SEQ_STEPS):
        firsts.append(
            remote(kv.at[n], kv.at[n], send.at[j], recv.at[j], seq_peer(dy, dx), head)
        )
    return firsts


def gather_start(kv, send, recv, fsend, frecv):
    for copy in gather_copies(kv, send, recv, fsend, frecv):
        copy.start()


def gather_finish(kv, send, recv, fsend, frecv):
    head = lax.axis_index("head")
    sib = seq_sibling()
    firsts = gather_copies(kv, send, recv, fsend, frecv)
    forwards = []
    for j, (dy, dx) in enumerate(SEQ_STEPS):
        src = seq_peer(-dy, dx)
        firsts[j + 1].wait_recv()
        forward = remote(kv.at[src], kv.at[src], fsend.at[j + 1], frecv.at[j + 1], sib, head)
        forward.start()
        forwards.append(forward)
    for copy in [firsts[0]] + forwards:
        copy.wait_recv()
    for copy in firsts + forwards:
        copy.wait_send()


def segment_of(place, lens_ref):
    end = jnp.int32(0)
    seg = jnp.zeros(place.shape, jnp.int32)
    for c in range(4):
        end = end + lens_ref[0, c]
        seg = seg + (place >= end).astype(jnp.int32)
    return seg


def prompt_of(seg, prompt_ref):
    out = jnp.zeros(seg.shape, jnp.int32)
    for c in range(4):
        out = jnp.where(seg == c, prompt_ref[0, c], out)
    return out


def load_keys(kv, k_r, v_r, kke, vve, kket):
    for r in range(8):
        rows = pl.ds(r * TOK, TOK)
        kke[rows, :HD] = kv[r, 0]
        kke[rows, HD:] = kv[8 + r, 0]
        vve[rows, :HD] = kv[r, 1]
        vve[rows, HD:] = kv[8 + r, 1]
    local = pl.ds(1024, 256)
    kke[local, :HD] = k_r[...]
    kke[local, HD:] = k_r[...]
    vve[local, :HD] = v_r[...]
    vve[local, HD:] = v_r[...]
    for r in range(10):
        rows = pl.ds(r * TOK, TOK)
        kket[:, rows] = kke[rows, :].T


def load_rows(q, do, col_prompt, qext, doext):
    first = col_prompt == 0
    zero = jnp.zeros((TOK, HD), BF16)
    first = jnp.broadcast_to(first, (TOK, HD))
    for h in range(GROUP):
        lanes = pl.ds(h * HD, HD)
        rows = pl.ds(h * TOK, TOK)
        qv, dov = q[:, lanes], do[:, lanes]
        qext[rows, :HD] = jnp.where(first, qv, zero)
        qext[rows, HD:] = jnp.where(first, zero, qv)
        doext[rows, :HD] = jnp.where(first, dov, zero)
        doext[rows, HD:] = jnp.where(first, zero, dov)


def fold(x, op):
    return op(x.reshape(TOK // 8, 8, x.shape[1]), axis=0)


def head_pair(hp, tiles, bias_of, qext, doext, kke, vve, s_ref, dp_ref, et, dst):
    rows = pl.ds(pl.multiple_of(hp * 256, 256), 256)
    qe, doe = qext[rows, :], doext[rows, :]
    top = jnp.full((8, 256), NEG, F32)
    for t in range(tiles):
        keys = pl.ds(t * TOK, TOK)
        s = dot(kke[keys, :], qe, NT)
        s = bias_of(t, s)
        s_ref[keys, :] = s
        top = jnp.maximum(top, fold(s, jnp.max))
        dp_ref[keys, :] = dot(vve[keys, :], doe, NT)
    top = jnp.max(top, axis=0, keepdims=True)
    norm = jnp.zeros((8, 256), F32)
    weighted = jnp.zeros((8, 256), F32)
    for t in range(tiles):
        keys = pl.ds(t * TOK, TOK)
        e = jnp.exp2((s_ref[keys, :] - top) * EXP2)
        s_ref[keys, :] = e
        norm = norm + fold(e, jnp.sum)
        weighted = weighted + fold(e * dp_ref[keys, :], jnp.sum)
    inv = 1.0 / jnp.sum(norm, axis=0, keepdims=True)
    mean = jnp.sum(weighted, axis=0, keepdims=True) * inv
    for t in range(tiles):
        keys = pl.ds(t * TOK, TOK)
        p = s_ref[keys, :] * inv
        et[keys, rows] = p.astype(BF16)
        dst[keys, rows] = (p * (dp_ref[keys, :] - mean)).astype(BF16)


def chunk_products(tiles, first, qext, doext, kket, et, dst, dkk, dvv):
    for t in range(tiles):
        keys = pl.ds(t * TOK, TOK)
        dv = dot(et[keys, :], doext[...], NN)
        dk = dot(dst[keys, :], qext[...], NN)
        if first:
            dvv[keys, :] = dv
            dkk[keys, :] = dk
        else:
            dvv[keys, :] += dv
            dkk[keys, :] += dk


def chunk_dq(tiles, row_prompt, kket, dst, dq_ref, rows_out):
    keys = pl.ds(0, tiles * TOK)
    first = row_prompt == 0
    for hp in range(4):
        rows = pl.ds(hp * 256, 256)
        both = dot(kket[:, keys], dst[keys, rows], NN)
        for k in range(2):
            lanes = slice(k * TOK, (k + 1) * TOK)
            part = jnp.where(first, both[:HD, lanes], both[HD:, lanes]) * SCALE
            h = hp * 2 + k
            dq_ref[rows_out, h * HD : (h + 1) * HD] = part.T.astype(BF16)


SIDES = (
    dict(give=(1, 3), keep=(0, 3), last=1),
    dict(give=(2, 4), keep=(1, 0), last=0),
)


def owner_of(offset, side):
    h = lax.axis_index("head")
    x, z = h // 4, lax.rem(h, 4)
    if offset == 0:
        oz = z
    elif offset == 1:
        oz = z + 1 - 2 * lax.rem(z, 2)
    elif offset == 2:
        oz = lax.rem(z + 2, 4)
    else:
        oz = 3 - z
    ox = x if side == 0 else 1 - x
    return ox * 4 + oz


WEIGHT_ORDER = (2, 1, 3, 0)


def weight_copies(offsets, w_q, w_k, w_v, w, sem):
    for offset in offsets:
        for side in range(2):
            rows = pl.ds(pl.multiple_of(owner_of(offset, side) * COLS, COLS), COLS)
            into = pl.ds(side * COLS, COLS)
            yield from [
                pltpu.make_async_copy(w_q.at[rows], w.at[offset, into, pl.ds(0, 1024)], sem.at[offset, side, 0]),
                pltpu.make_async_copy(w_k.at[rows], w.at[offset, into, pl.ds(1024, HD)], sem.at[offset, side, 1]),
                pltpu.make_async_copy(w_v.at[rows], w.at[offset, into, pl.ds(1152, HD)], sem.at[offset, side, 2]),
            ]


class HeadSum:
    def __init__(self, chunk, terms, r1, s2, r2, s3, r3, sems):
        self.chunk = chunk
        self.terms, self.r1, self.s2, self.r2, self.s3, self.r3 = (
            terms.at[chunk], r1.at[chunk], s2.at[chunk], r2.at[chunk], s3.at[chunk], r3.at[chunk]
        )
        self.sems = sems
        self.seq = lax.axis_index("seq")
        self.z1, self.z3, self.flip = head_peers()

    def copy(self, half, step):
        send, recv = (self.sems.at[k, self.chunk, half, step] for k in range(2))
        near, far = (self.z1, self.z3) if half == 0 else (self.z3, self.z1)
        if step == 0:
            low, high = SIDES[half]["give"]
            src = self.terms.at[pl.ds(low, high - low), :, pl.ds(half * 64, 64), :]
            return remote(src, self.r1.at[half], send, recv, self.seq, near)
        if step == 1:
            return remote(self.s2.at[half], self.r2.at[half], send, recv, self.seq, self.flip)
        return remote(self.s3.at[half], self.r3.at[half], send, recv, self.seq, far)

    def first(self, half):
        self.copy(half, 0).start()

    def second(self, half):
        self.copy(half, 0).wait_recv()
        rows = slice(half * 64, half * 64 + 64)
        for k, offset in enumerate(SIDES[half]["keep"]):
            total = self.terms[offset, 1, rows, :].astype(F32) + self.r1[half, k, 1].astype(F32)
            self.s2[half, k] = total.astype(BF16)
        self.copy(half, 1).start()

    def kept(self, half, k):
        rows = slice(half * 64, half * 64 + 64)
        offset = SIDES[half]["keep"][k]
        return (
            self.terms[offset, 0, rows, :].astype(F32)
            + self.r1[half, k, 0].astype(F32)
            + self.r2[half, k].astype(F32)
        )

    def third(self, half):
        self.copy(half, 1).wait_recv()
        self.s3[half] = self.kept(half, SIDES[half]["last"]).astype(BF16)
        self.copy(half, 2).start()

    def final(self, half, out, base):
        total = self.kept(half, 1 - SIDES[half]["last"])
        self.copy(half, 2).wait_recv()
        out[base + half * 64 : base + half * 64 + 64, :] = (
            total + self.r3[half].astype(F32)
        ).astype(BF16)

    def drain(self):
        for half in range(2):
            for step in range(3):
                self.copy(half, step).wait_send()


def store_terms(block, terms, chunk, offset, part):
    for piece in range(2):
        side, lane = divmod(part * 256 + piece * 128, COLS)
        terms[chunk, offset, side, :, lane : lane + 128] = block[:, piece * 128 : piece * 128 + 128]


def project(d, w, terms, chunk, wait_weights):
    rows = d[...]
    for offset in WEIGHT_ORDER:
        if wait_weights is not None:
            wait_weights(offset)
        for part in range(5):
            block = dot(rows, w[offset, part * 256 : (part + 1) * 256, :], NT)
            store_terms(block.astype(BF16), terms, chunk, offset, part)


def project_early(d, w, early):
    rows = d[:, :1024]
    for offset in WEIGHT_ORDER:
        for part in range(5):
            cols = slice(part * 256, (part + 1) * 256)
            early[offset, :, cols] = dot(rows, w[offset, cols, :1024], NT)


def project_late(d, w, early, terms, chunk):
    rows = d[:, 1024:]
    for offset in WEIGHT_ORDER:
        for part in range(5):
            cols = slice(part * 256, (part + 1) * 256)
            block = early[offset, :, cols] + dot(rows, w[offset, cols, 1024:], NT)
            store_terms(block.astype(BF16), terms, chunk, offset, part)


def grads_sibling(grads, rc, gsem):
    c = lax.rem(lax.axis_index("seq"), 2)
    return remote(
        grads.at[:, 1 - c], rc, gsem.at[0, 7], gsem.at[1, 7], seq_sibling(), lax.axis_index("head")
    )


def grads_copies(gs, rg, gsem):
    y, x, c = seq_place()
    copies = []
    for j, (dy, dx) in enumerate(SEQ_STEPS):
        oy = lax.rem(y + dy, 4)
        ox = lax.rem(x + dx, 2)
        block = lax.rem(oy, 2) * 2 + ox
        copies.append(
            remote(
                gs.at[block, oy // 2], rg.at[j], gsem.at[0, j], gsem.at[1, j],
                seq_peer(dy, dx), lax.axis_index("head"),
            )
        )
    return copies


def grads_second(grads, rc, gs, rg, gsem):
    c = lax.rem(lax.axis_index("seq"), 2)
    grads_sibling(grads, rc, gsem).wait_recv()
    for b in range(4):
        for p in range(2):
            gs[b, p] = (grads[b, c, p].astype(F32) + rc[b, p].astype(F32)).astype(BF16)
    for copy in grads_copies(gs, rg, gsem):
        copy.start()


def grads_finish(gs, rg, gsem, d_p):
    y, x, c = seq_place()
    total = gs[lax.rem(y, 2) * 2 + x, y // 2].astype(F32)
    for j, copy in enumerate(grads_copies(gs, rg, gsem)):
        copy.wait_recv()
        total = total + rg[j].astype(F32)
    d_p[:, 1024:] = total.astype(BF16)


def whole_kernel(
    lens_ref, prompt_ref, q_p_h, k_p_h, v_p_h, do_p_h, q_r_h, k_r_h, v_r_h, do_r_h, w_q, w_k, w_v,
    out_p, out_r,
    kv, q_p, do_p, q_r, do_r, k_r, v_r,
    kke, vve, kket, qext, doext, s_ref, dp_ref, et, dst, dkk, dvv, bias, d_r, d_p, grads, early,
    w, terms, r1, s2, r2, s3, r3, rc, gs, rg,
    lsem, send, recv, fsend, frecv, wsem, hsem, gsem,
):
    seq, head = lax.axis_index("seq"), lax.axis_index("head")
    barrier = pltpu.get_barrier_semaphore()
    seqs = [seq_sibling()] + [seq_peer(dy, dx) for dy, dx in SEQ_STEPS]
    heads = list(head_peers())
    for peer in seqs:
        pl.semaphore_signal(barrier, inc=1, device_id=(peer, head), device_id_type=MESH)
    for peer in heads:
        pl.semaphore_signal(barrier, inc=1, device_id=(seq, peer), device_id_type=MESH)
    loads = [
        pltpu.make_async_copy(src, dst_ref, lsem.at[k])
        for k, (src, dst_ref) in enumerate((
            (k_p_h, kv.at[seq, 0]), (v_p_h, kv.at[seq, 1]), (q_r_h, q_r), (do_r_h, do_r),
            (k_r_h, k_r), (v_r_h, v_r), (q_p_h, q_p), (do_p_h, do_p),
        ))
    ]
    for copy in loads:
        copy.start()
    for copy in loads[:2]:
        copy.wait()
    pl.semaphore_wait(barrier, len(seqs) + len(heads))
    gather_start(kv, send, recv, fsend, frecv)
    for copy in weight_copies(WEIGHT_ORDER, w_q, w_k, w_v, w, wsem):
        copy.start()
    for copy in loads[2:]:
        copy.wait()
    sums = [HeadSum(c, terms, r1, s2, r2, s3, r3, hsem) for c in range(3)]

    def response(half, first):
        tiles = 8 + half + 1
        count = (half + 1) * TOK
        base = half * TOK
        col = base + lax.broadcasted_iota(jnp.int32, (TOK, 1), 0)
        col_prompt = prompt_of(segment_of(col, lens_ref), prompt_ref)
        row = base + lax.rem(lax.broadcasted_iota(jnp.int32, (1, 256), 1), TOK)
        row_seg = segment_of(row, lens_ref)
        row_prompt = prompt_of(row_seg[:, :TOK], prompt_ref)
        key = lax.broadcasted_iota(jnp.int32, (count, 1), 0)
        key_seg = segment_of(key, lens_ref)
        seen = (key_seg == row_seg) & (key <= row)
        bias[:count, :] = jnp.where(seen, 0.0, NEG)
        span = slice(base, base + TOK)
        load_rows(q_r.at[span], do_r.at[span], col_prompt, qext, doext)
        if first:
            gather_finish(kv, send, recv, fsend, frecv)
            load_keys(kv, k_r, v_r, kke, vve, kket)

        def local_bias(t, s):
            if t < 8:
                return s
            return s + bias[(t - 8) * TOK : (t - 7) * TOK, :]

        def visit(hp, c):
            head_pair(
                hp, tiles, local_bias, qext, doext, kke, vve, s_ref, dp_ref, et, dst
            )
            return c

        lax.fori_loop(0, 4, visit, 0)
        chunk_products(tiles, first, qext, doext, kket, et, dst, dkk, dvv)
        chunk_dq(tiles, row_prompt, kket, dst, d_r, span)
        local = slice(1024 + base, 1024 + base + TOK)
        d_r[span, 1024:1152] = ((dkk[local, :HD] + dkk[local, HD:]) * SCALE).astype(BF16)
        d_r[span, 1152:] = (dvv[local, :HD] + dvv[local, HD:]).astype(BF16)

    def wait_weights(offset):
        for copy in weight_copies((offset,), w_q, w_k, w_v, w, wsem):
            copy.wait()

    def both(step, chunk):
        for half in range(2):
            step(sums[chunk], half)

    response(1, True)
    project(d_r.at[TOK:256], w, terms, 1, wait_weights)
    both(HeadSum.first, 1)
    response(0, False)
    both(HeadSum.second, 1)

    place = lax.rem(seq, 8) * TOK
    diff = (
        place
        + lax.rem(lax.broadcasted_iota(jnp.int32, (TOK, 256), 1), TOK)
        - lax.broadcasted_iota(jnp.int32, (TOK, 256), 0)
    )
    mine = seq // 8
    load_rows(q_p, do_p, jnp.full((TOK, 1), mine, jnp.int32), qext, doext)

    def causal(t, s):
        return jnp.where(diff >= t * TOK, s, NEG)

    def visit(hp, c):
        head_pair(hp, 8, causal, qext, doext, kke, vve, s_ref, dp_ref, et, dst)
        return c

    lax.fori_loop(0, 4, visit, 0)
    chunk_products(8, False, qext, doext, kket, et, dst, dkk, dvv)
    for r in range(8):
        keys = slice(r * TOK, (r + 1) * TOK)
        for p in range(2):
            lanes = slice(p * HD, (p + 1) * HD)
            grads[r // 2, r % 2, p, :, :HD] = (dkk[keys, lanes] * SCALE).astype(BF16)
            grads[r // 2, r % 2, p, :, HD:] = dvv[keys, lanes].astype(BF16)
    grads_sibling(grads, rc, gsem).start()
    both(HeadSum.third, 1)
    chunk_dq(8, jnp.full((1, TOK), mine, jnp.int32), kket, dst, d_p, slice(0, TOK))
    grads_second(grads, rc, gs, rg, gsem)
    project(d_r.at[0:TOK], w, terms, 0, None)
    both(HeadSum.first, 0)
    project_early(d_p, w, early)
    both(HeadSum.second, 0)
    grads_finish(gs, rg, gsem, d_p)
    project_late(d_p, w, early, terms, 2)
    both(HeadSum.first, 2)
    both(HeadSum.third, 0)
    for half in range(2):
        sums[1].final(half, out_r, TOK)
    both(HeadSum.second, 2)
    for half in range(2):
        sums[0].final(half, out_r, 0)
    both(HeadSum.third, 2)
    for half in range(2):
        sums[2].final(half, out_p, 0)
    grads_sibling(grads, rc, gsem).wait_send()
    for copy in grads_copies(gs, rg, gsem):
        copy.wait_send()
    for c in range(3):
        sums[c].drain()


def shards(
    q_prompt, k_prompt, v_prompt, do_prompt, q_resp, k_resp, v_resp, do_resp,
    resp_lengths, resp_prompt, w_query, w_key, w_value,
):
    whole = pl.BlockSpec(memory_space=VMEM)
    hbm = pl.BlockSpec(memory_space=pl.ANY)
    scalars = pl.BlockSpec(memory_space=pltpu.SMEM)
    return pl.pallas_call(
        whole_kernel,
        out_shape=(
            jax.ShapeDtypeStruct((TOK, COLS), BF16),
            jax.ShapeDtypeStruct((256, COLS), BF16),
        ),
        in_specs=[scalars] * 2 + [hbm] * 11,
        out_specs=(whole,) * 2,
        scratch_shapes=[
            VMEM((16, 2, TOK, HD), BF16),
            VMEM((TOK, 1024), BF16),
            VMEM((TOK, 1024), BF16),
            VMEM((256, 1024), BF16),
            VMEM((256, 1024), BF16),
            VMEM((256, HD), BF16),
            VMEM((256, HD), BF16),
            VMEM((WIDE, 256), BF16),
            VMEM((WIDE, 256), BF16),
            VMEM((256, WIDE), BF16),
            VMEM((1024, 256), BF16),
            VMEM((1024, 256), BF16),
            VMEM((WIDE, 256), F32),
            VMEM((WIDE, 256), F32),
            VMEM((WIDE, 1024), BF16),
            VMEM((WIDE, 1024), BF16),
            VMEM((WIDE, 256), F32),
            VMEM((WIDE, 256), F32),
            VMEM((256, 256), F32),
            VMEM((256, WIDE), BF16),
            VMEM((TOK, WIDE), BF16),
            VMEM((4, 2, 2, TOK, 256), BF16),
            VMEM((4, TOK, WIDE), F32),
            VMEM((4, WIDE, WIDE), BF16),
            VMEM((3, 4, 2, TOK, COLS), BF16),
            VMEM((3, 2, 2, 2, 64, COLS), BF16),
            VMEM((3, 2, 2, 64, COLS), BF16),
            VMEM((3, 2, 2, 64, COLS), BF16),
            VMEM((3, 2, 64, COLS), BF16),
            VMEM((3, 2, 64, COLS), BF16),
            VMEM((4, 2, TOK, 256), BF16),
            VMEM((4, 2, TOK, 256), BF16),
            VMEM((7, TOK, 256), BF16),
            pltpu.SemaphoreType.DMA((8,)),
            pltpu.SemaphoreType.DMA((7,)),
            pltpu.SemaphoreType.DMA((7,)),
            pltpu.SemaphoreType.DMA((8,)),
            pltpu.SemaphoreType.DMA((8,)),
            pltpu.SemaphoreType.DMA((4, 2, 3)),
            pltpu.SemaphoreType.DMA((2, 3, 2, 3)),
            pltpu.SemaphoreType.DMA((2, 8)),
        ],
        compiler_params=pltpu.CompilerParams(
            collective_id=0, has_side_effects=True, vmem_limit_bytes=60 << 20
        ),
        name="attention_back",
    )(
        resp_lengths, resp_prompt, q_prompt, k_prompt, v_prompt, do_prompt,
        q_resp, k_resp, v_resp, do_resp, w_query, w_key, w_value,
    )


def solution(mesh):
    return jax.shard_map(
        shards,
        mesh=mesh,
        in_specs=(P("seq", "head"),) * 8 + (P("seq", None),) * 2 + (P(None, "head"),) * 3,
        out_specs=(P("seq", "head"), P("seq", "head")),
        check_vma=False,
    )
```

time: 106 us -> 92.5 us (0.87)
  local copies, waits for them, and re-layouts: 12.3 us -> 3.32 us
  Pallas kernels: 92.4 us -> 88.3 us
    unnamed x28 -> x2, local copies, waits for them, and re-layouts: 12.3 us -> 3.32 us
    pallas_call x3 -> x1, Pallas kernels: 92.4 us -> 88.3 us  [shards(): pl.pallas_call(whole_kernel, out_shape=(jax.ShapeDtypeStruct((TOK, COLS),...]
where the time goes in v2:
time: 92.5 us; the launch traced here: 92.3 us
  Pallas kernels  88.3 us (95%)
  local copies, waits for them, and re-layouts  3.32 us (4%)
    pallas_call x1, Pallas kernels, shards(): pl.pallas_call(whole_kernel, out_shape=(jax.ShapeDtypeStruct((TOK, COLS),...  88.3 us
    unnamed x2, local copies, waits for them, and re-layouts  3.32 us

profile of v2, /device:TPU:0, one launch (start us, length us, event | category | flops | bytes accessed | tf_op | source)
XLA Modules:
  0.0 92.3 jit_solution(7580816708295862149)
XLA Ops:
  0.6 88.3 %attention_back.1 = (bf16[128,640]{1,0:T(8,128)(2,1)}, bf16[256,640]{1,0:T(8,128)(2,1)}) custom-call(s32[1,4]{1,0:T(1,128)} %lens_ref.1, s32[1,4]{1,0:T(1,128)} %prompt_ref.1, bf16[128,1024]{1,0:T(8,128)(2,1)} %q_p_h.1, bf16[128,128]{1,0:T(8,128)(2,1)} %k_p_h.1, bf16[128,128]{1,0:T(8,128)(2,1)} %v_p_h.1, bf16[128,1024]{1,0:T(8,128)(2,1)} %do_p_h.1, ...), custom_call_target="tpu_custom_call" | custom-call | tf_op jit(solution)/shard_map/attention_back/pallas_call | solution.py:520
  89.0 1.6 %copy.17 = bf16[128,640]{1,0:T(8,128)(2,1)} copy(bf16[128,640]{1,0:T(8,128)(2,1)} %get-tuple-element.4) | data formatting | bytes 327680
  90.6 1.7 %copy.18 = bf16[256,640]{1,0:T(8,128)(2,1)} copy(bf16[256,640]{1,0:T(8,128)(2,1)} %get-tuple-element.5) | data formatting | bytes 655360

commit v3 on v2

--- a/solution.py
+++ b/solution.py
@@ -20,6 +20,7 @@
 EXP2 = SCALE * math.log2(math.e)
 D = 5120
 COLS = 640
+HALF = 320
 WIDE = 1280
 NT = (((1,), (1,)), ((), ()))
 NN = (((1,), (0,)), ((), ()))
@@ -113,7 +114,7 @@
     return out
 
 
-def load_keys(kv, k_r, v_r, kke, vve, kket):
+def load_keys(kv, k_r, v_r, kke, vve):
     for r in range(8):
         rows = pl.ds(r * TOK, TOK)
         kke[rows, :HD] = kv[r, 0]
@@ -125,6 +126,9 @@
     kke[local, HD:] = k_r[...]
     vve[local, :HD] = v_r[...]
     vve[local, HD:] = v_r[...]
+
+
+def turn_keys(kke, kket):
     for r in range(10):
         rows = pl.ds(r * TOK, TOK)
         kket[:, rows] = kke[rows, :].T
@@ -145,57 +149,79 @@
 
 
 def fold(x, op):
-    return op(x.reshape(TOK // 8, 8, x.shape[1]), axis=0)
-
-
-def head_pair(hp, tiles, bias_of, qext, doext, kke, vve, s_ref, dp_ref, et, dst):
-    rows = pl.ds(pl.multiple_of(hp * 256, 256), 256)
-    qe, doe = qext[rows, :], doext[rows, :]
-    top = jnp.full((8, 256), NEG, F32)
-    for t in range(tiles):
-        keys = pl.ds(t * TOK, TOK)
-        s = dot(kke[keys, :], qe, NT)
-        s = bias_of(t, s)
-        s_ref[keys, :] = s
-        top = jnp.maximum(top, fold(s, jnp.max))
-        dp_ref[keys, :] = dot(vve[keys, :], doe, NT)
-    top = jnp.max(top, axis=0, keepdims=True)
-    norm = jnp.zeros((8, 256), F32)
-    weighted = jnp.zeros((8, 256), F32)
-    for t in range(tiles):
-        keys = pl.ds(t * TOK, TOK)
-        e = jnp.exp2((s_ref[keys, :] - top) * EXP2)
-        s_ref[keys, :] = e
-        norm = norm + fold(e, jnp.sum)
-        weighted = weighted + fold(e * dp_ref[keys, :], jnp.sum)
-    inv = 1.0 / jnp.sum(norm, axis=0, keepdims=True)
-    mean = jnp.sum(weighted, axis=0, keepdims=True) * inv
-    for t in range(tiles):
-        keys = pl.ds(t * TOK, TOK)
-        p = s_ref[keys, :] * inv
-        et[keys, rows] = p.astype(BF16)
-        dst[keys, rows] = (p * (dp_ref[keys, :] - mean)).astype(BF16)
-
-
-def chunk_products(tiles, first, qext, doext, kket, et, dst, dkk, dvv):
-    for t in range(tiles):
-        keys = pl.ds(t * TOK, TOK)
-        dv = dot(et[keys, :], doext[...], NN)
-        dk = dot(dst[keys, :], qext[...], NN)
+    return op(x.reshape(x.shape[0] // 8, 8, x.shape[1]), axis=0)
+
+
+def key_groups(keys):
+    size = 256
+    return [(k, min(size, keys - k)) for k in range(0, keys, size)]
+
+
+def chunk_scores(keys, bias_of, qext, doext, kke, vve, s_refs, dp_refs, et, dst):
+    low = jnp.full((8, 256), NEG, F32)
+
+    def scores(hp, group, top):
+        start, size = group
+        s = dot(kke[start : start + size, :], qext[hp * 256 : hp * 256 + 256, :], NT)
+        for j in range(0, size, TOK):
+            tile = bias_of((start + j) // TOK, s[j : j + TOK])
+            s_refs[hp % 2][start + j : start + j + TOK, :] = tile
+            top = jnp.maximum(top, fold(tile, jnp.max))
+        return top
+
+    def grads(hp, group):
+        span = slice(group[0], group[0] + group[1])
+        dp_refs[hp % 2][span, :] = dot(vve[span, :], doext[hp * 256 : hp * 256 + 256, :], NT)
+
+    def tiles(group):
+        return [slice(j, j + TOK) for j in range(group[0], group[0] + group[1], TOK)]
+
+    groups = key_groups(keys)
+    top = low
+    for group in groups:
+        top = scores(0, group, top)
+        grads(0, group)
+    for hp in range(4):
+        s_ref, dp_ref = s_refs[hp % 2], dp_refs[hp % 2]
+        cols = slice(hp * 256, hp * 256 + 256)
+        top = jnp.max(top, axis=0, keepdims=True)
+        norm = jnp.zeros((8, 256), F32)
+        weighted = jnp.zeros((8, 256), F32)
+        next_top = low
+        for group in groups:
+            if hp < 3:
+                next_top = scores(hp + 1, group, next_top)
+            for span in tiles(group):
+                e = jnp.exp2((s_ref[span, :] - top) * EXP2)
+                s_ref[span, :] = e
+                norm = norm + fold(e, jnp.sum)
+                weighted = weighted + fold(e * dp_ref[span, :], jnp.sum)
+        inv = 1.0 / jnp.sum(norm, axis=0, keepdims=True)
+        mean = jnp.sum(weighted, axis=0, keepdims=True) * inv
+        for group in groups:
+            if hp < 3:
+                grads(hp + 1, group)
+            for span in tiles(group):
+                p = s_ref[span, :] * inv
+                et[span, cols] = p.astype(BF16)
+                dst[span, cols] = (p * (dp_ref[span, :] - mean)).astype(BF16)
+        top = next_top
+
+
+def chunk_product(keys, first, left, right, total):
+    for start, size in key_groups(keys):
+        span = slice(start, start + size)
+        value = dot(left[span, :], right[...], NN)
         if first:
-            dvv[keys, :] = dv
-            dkk[keys, :] = dk
+            total[span, :] = value
         else:
-            dvv[keys, :] += dv
-            dkk[keys, :] += dk
-
-
-def chunk_dq(tiles, row_prompt, kket, dst, dq_ref, rows_out):
-    keys = pl.ds(0, tiles * TOK)
+            total[span, :] += value
+
+
+def chunk_dq(keys, row_prompt, kket, dst, dq_ref, rows_out):
     first = row_prompt == 0
     for hp in range(4):
-        rows = pl.ds(hp * 256, 256)
-        both = dot(kket[:, keys], dst[keys, rows], NN)
+        both = dot(kket[:, :keys], dst[:keys, hp * 256 : hp * 256 + 256], NN)
         for k in range(2):
             lanes = slice(k * TOK, (k + 1) * TOK)
             part = jnp.where(first, both[:HD, lanes], both[HD:, lanes]) * SCALE
@@ -240,11 +266,12 @@
 
 
 class HeadSum:
-    def __init__(self, chunk, terms, r1, s2, r2, s3, r3, sems):
+    def __init__(self, chunk, terms, r1, s2, r2, s3, r3, sums, sems):
         self.chunk = chunk
         self.terms, self.r1, self.s2, self.r2, self.s3, self.r3 = (
             terms.at[chunk], r1.at[chunk], s2.at[chunk], r2.at[chunk], s3.at[chunk], r3.at[chunk]
         )
+        self.sums = sums.at[chunk]
         self.sems = sems
         self.seq = lax.axis_index("seq")
         self.z1, self.z3, self.flip = head_peers()
@@ -252,83 +279,75 @@
     def copy(self, half, step):
         send, recv = (self.sems.at[k, self.chunk, half, step] for k in range(2))
         near, far = (self.z1, self.z3) if half == 0 else (self.z3, self.z1)
-        if step == 0:
+        if step < 2:
+            side = 1 - step
             low, high = SIDES[half]["give"]
-            src = self.terms.at[pl.ds(low, high - low), :, pl.ds(half * 64, 64), :]
-            return remote(src, self.r1.at[half], send, recv, self.seq, near)
-        if step == 1:
-            return remote(self.s2.at[half], self.r2.at[half], send, recv, self.seq, self.flip)
+            src = self.terms.at[pl.ds(low, high - low), half, side]
+            return remote(src, self.r1.at[half, side], send, recv, self.seq, near)
+        if step < 4:
+            k = step - 2
+            return remote(self.s2.at[half, k], self.r2.at[half, k], send, recv, self.seq, self.flip)
         return remote(self.s3.at[half], self.r3.at[half], send, recv, self.seq, far)
 
     def first(self, half):
         self.copy(half, 0).start()
+        self.copy(half, 1).start()
 
     def second(self, half):
         self.copy(half, 0).wait_recv()
-        rows = slice(half * 64, half * 64 + 64)
-        for k, offset in enumerate(SIDES[half]["keep"]):
-            total = self.terms[offset, 1, rows, :].astype(F32) + self.r1[half, k, 1].astype(F32)
+        last = SIDES[half]["last"]
+        for k in (last, 1 - last):
+            offset = SIDES[half]["keep"][k]
+            total = self.terms[offset, half, 1].astype(F32) + self.r1[half, 1, k].astype(F32)
             self.s2[half, k] = total.astype(BF16)
-        self.copy(half, 1).start()
+            self.copy(half, 2 + k).start()
 
     def kept(self, half, k):
-        rows = slice(half * 64, half * 64 + 64)
+        self.copy(half, 2 + k).wait_recv()
         offset = SIDES[half]["keep"][k]
         return (
-            self.terms[offset, 0, rows, :].astype(F32)
-            + self.r1[half, k, 0].astype(F32)
+            self.terms[offset, half, 0].astype(F32)
+            + self.r1[half, 0, k].astype(F32)
             + self.r2[half, k].astype(F32)
         )
 
     def third(self, half):
         self.copy(half, 1).wait_recv()
         self.s3[half] = self.kept(half, SIDES[half]["last"]).astype(BF16)
-        self.copy(half, 2).start()
-
-    def final(self, half, out, base):
+        self.copy(half, 4).start()
+
+    def final(self, half):
         total = self.kept(half, 1 - SIDES[half]["last"])
-        self.copy(half, 2).wait_recv()
-        out[base + half * 64 : base + half * 64 + 64, :] = (
-            total + self.r3[half].astype(F32)
-        ).astype(BF16)
+        self.copy(half, 4).wait_recv()
+        self.sums[half * HALF : (half + 1) * HALF, :] = total + self.r3[half].astype(F32)
+
+    def write(self, out, base):
+        for part in range(5):
+            lanes = slice(part * TOK, (part + 1) * TOK)
+            out[base : base + TOK, lanes] = self.sums[lanes, :].T.astype(BF16)
 
     def drain(self):
         for half in range(2):
-            for step in range(3):
+            for step in range(5):
                 self.copy(half, step).wait_send()
 
 
-def store_terms(block, terms, chunk, offset, part):
-    for piece in range(2):
-        side, lane = divmod(part * 256 + piece * 128, COLS)
-        terms[chunk, offset, side, :, lane : lane + 128] = block[:, piece * 128 : piece * 128 + 128]
-
-
-def project(d, w, terms, chunk, wait_weights):
-    rows = d[...]
+BLOCKS = ((1, 0), (1, 1), (0, 0), (0, 1))
+
+
+def block_rows(side, half):
+    start = side * COLS + half * HALF
+    return slice(start, start + HALF)
+
+
+def project(rows, w, put, wait_weights, started):
     for offset in WEIGHT_ORDER:
         if wait_weights is not None:
             wait_weights(offset)
-        for part in range(5):
-            block = dot(rows, w[offset, part * 256 : (part + 1) * 256, :], NT)
-            store_terms(block.astype(BF16), terms, chunk, offset, part)
-
-
-def project_early(d, w, early):
-    rows = d[:, :1024]
-    for offset in WEIGHT_ORDER:
-        for part in range(5):
-            cols = slice(part * 256, (part + 1) * 256)
-            early[offset, :, cols] = dot(rows, w[offset, cols, :1024], NT)
-
-
-def project_late(d, w, early, terms, chunk):
-    rows = d[:, 1024:]
-    for offset in WEIGHT_ORDER:
-        for part in range(5):
-            cols = slice(part * 256, (part + 1) * 256)
-            block = early[offset, :, cols] + dot(rows, w[offset, cols, 1024:], NT)
-            store_terms(block.astype(BF16), terms, chunk, offset, part)
+        for side, half in BLOCKS:
+            put(offset, half, side, dot(w[offset, block_rows(side, half), :], rows, NT))
+        if offset in started:
+            started[offset]()
 
 
 def grads_sibling(grads, rc, gsem):
@@ -370,15 +389,15 @@
     for j, copy in enumerate(grads_copies(gs, rg, gsem)):
         copy.wait_recv()
         total = total + rg[j].astype(F32)
-    d_p[:, 1024:] = total.astype(BF16)
+    d_p[...] = total.astype(BF16)
 
 
 def whole_kernel(
     lens_ref, prompt_ref, q_p_h, k_p_h, v_p_h, do_p_h, q_r_h, k_r_h, v_r_h, do_r_h, w_q, w_k, w_v,
     out_p, out_r,
     kv, q_p, do_p, q_r, do_r, k_r, v_r,
-    kke, vve, kket, qext, doext, s_ref, dp_ref, et, dst, dkk, dvv, bias, d_r, d_p, grads, early,
-    w, terms, r1, s2, r2, s3, r3, rc, gs, rg,
+    kke, vve, kket, qext, doext, s0, s1, dp0, dp1, et, dst, dkk, dvv, bias0, bias1, d_b, d_ap, late, grads, early,
+    w, terms, r1, s2, r2, s3, r3, totals, rc, gs, rg,
     lsem, send, recv, fsend, frecv, wsem, hsem, gsem,
 ):
     seq, head = lax.axis_index("seq"), lax.axis_index("head")
@@ -406,44 +425,58 @@
         copy.start()
     for copy in loads[2:]:
         copy.wait()
-    sums = [HeadSum(c, terms, r1, s2, r2, s3, r3, hsem) for c in range(3)]
-
-    def response(half, first):
-        tiles = 8 + half + 1
-        count = (half + 1) * TOK
+    sums = [HeadSum(c, terms, r1, s2, r2, s3, r3, totals, hsem) for c in range(3)]
+    mine = seq // 8
+
+    row_prompts = []
+    for half, bias in ((0, bias0), (1, bias1)):
         base = half * TOK
         col = base + lax.broadcasted_iota(jnp.int32, (TOK, 1), 0)
-        col_prompt = prompt_of(segment_of(col, lens_ref), prompt_ref)
         row = base + lax.rem(lax.broadcasted_iota(jnp.int32, (1, 256), 1), TOK)
         row_seg = segment_of(row, lens_ref)
-        row_prompt = prompt_of(row_seg[:, :TOK], prompt_ref)
-        key = lax.broadcasted_iota(jnp.int32, (count, 1), 0)
+        row_prompts.append(prompt_of(row_seg[:, :TOK], prompt_ref))
+        key = lax.broadcasted_iota(jnp.int32, (base + TOK, 1), 0)
         key_seg = segment_of(key, lens_ref)
         seen = (key_seg == row_seg) & (key <= row)
-        bias[:count, :] = jnp.where(seen, 0.0, NEG)
+        bias[...] = jnp.where(seen, 0.0, NEG)
         span = slice(base, base + TOK)
-        load_rows(q_r.at[span], do_r.at[span], col_prompt, qext, doext)
-        if first:
-            gather_finish(kv, send, recv, fsend, frecv)
-            load_keys(kv, k_r, v_r, kke, vve, kket)
+        load_rows(
+            q_r.at[span], do_r.at[span], prompt_of(segment_of(col, lens_ref), prompt_ref),
+            qext.at[half], doext.at[half],
+        )
+    load_rows(q_p, do_p, jnp.full((TOK, 1), mine, jnp.int32), qext.at[2], doext.at[2])
+    diff = (
+        lax.rem(seq, 8) * TOK
+        + lax.rem(lax.broadcasted_iota(jnp.int32, (TOK, 256), 1), TOK)
+        - lax.broadcasted_iota(jnp.int32, (TOK, 256), 0)
+    )
+    d_ap[TOK:, 1024:] = jnp.zeros((TOK, 256), BF16)
+    gather_finish(kv, send, recv, fsend, frecv)
+    load_keys(kv, k_r, v_r, kke, vve)
+
+    def scores(keys, bias_of, chunk):
+        chunk_scores(
+            keys, bias_of, qext.at[chunk], doext.at[chunk], kke, vve, (s0, s1), (dp0, dp1), et, dst
+        )
+
+    def response(half, first, d_ref):
+        bias = (bias0, bias1)[half]
+        keys = 1024 + (half + 1) * TOK
 
         def local_bias(t, s):
             if t < 8:
                 return s
             return s + bias[(t - 8) * TOK : (t - 7) * TOK, :]
 
-        def visit(hp, c):
-            head_pair(
-                hp, tiles, local_bias, qext, doext, kke, vve, s_ref, dp_ref, et, dst
-            )
-            return c
-
-        lax.fori_loop(0, 4, visit, 0)
-        chunk_products(tiles, first, qext, doext, kket, et, dst, dkk, dvv)
-        chunk_dq(tiles, row_prompt, kket, dst, d_r, span)
-        local = slice(1024 + base, 1024 + base + TOK)
-        d_r[span, 1024:1152] = ((dkk[local, :HD] + dkk[local, HD:]) * SCALE).astype(BF16)
-        d_r[span, 1152:] = (dvv[local, :HD] + dvv[local, HD:]).astype(BF16)
+        scores(keys, local_bias, half)
+        if first:
+            turn_keys(kke, kket)
+        chunk_product(keys, first, et, doext.at[half], dvv)
+        chunk_product(keys, first, dst, qext.at[half], dkk)
+        chunk_dq(keys, row_prompts[half], kket, dst, d_ref, slice(0, TOK))
+        local = slice(1024 + half * TOK, 1024 + half * TOK + TOK)
+        d_ref[:TOK, 1024:1152] = ((dkk[local, :HD] + dkk[local, HD:]) * SCALE).astype(BF16)
+        d_ref[:TOK, 1152:] = (dvv[local, :HD] + dvv[local, HD:]).astype(BF16)
 
     def wait_weights(offset):
         for copy in weight_copies((offset,), w_q, w_k, w_v, w, wsem):
@@ -453,30 +486,24 @@
         for half in range(2):
             step(sums[chunk], half)
 
-    response(1, True)
-    project(d_r.at[TOK:256], w, terms, 1, wait_weights)
-    both(HeadSum.first, 1)
-    response(0, False)
+    def starts(chunk):
+        return {1: lambda: sums[chunk].first(0), 3: lambda: sums[chunk].first(1)}
+
+    def put_b(offset, half, side, value):
+        terms[1, offset, half, side] = value.astype(BF16)
+
+    def put_ap(offset, half, side, value):
+        terms[0, offset, half, side] = value[:, :TOK].astype(BF16)
+        early[offset, half, side] = value[:, TOK:]
+
+    response(1, True, d_b)
+    project(d_b[...], w, put_b, wait_weights, starts(1))
+    response(0, False, d_ap)
     both(HeadSum.second, 1)
 
-    place = lax.rem(seq, 8) * TOK
-    diff = (
-        place
-        + lax.rem(lax.broadcasted_iota(jnp.int32, (TOK, 256), 1), TOK)
-        - lax.broadcasted_iota(jnp.int32, (TOK, 256), 0)
-    )
-    mine = seq // 8
-    load_rows(q_p, do_p, jnp.full((TOK, 1), mine, jnp.int32), qext, doext)
-
-    def causal(t, s):
-        return jnp.where(diff >= t * TOK, s, NEG)
-
-    def visit(hp, c):
-        head_pair(hp, 8, causal, qext, doext, kke, vve, s_ref, dp_ref, et, dst)
-        return c
-
-    lax.fori_loop(0, 4, visit, 0)
-    chunk_products(8, False, qext, doext, kket, et, dst, dkk, dvv)
+    scores(1024, lambda t, s: jnp.where(diff >= t * TOK, s, NEG), 2)
+    chunk_product(1024, False, et, doext.at[2], dvv)
+    chunk_product(1024, False, dst, qext.at[2], dkk)
     for r in range(8):
         keys = slice(r * TOK, (r + 1) * TOK)
         for p in range(2):
@@ -484,25 +511,28 @@
             grads[r // 2, r % 2, p, :, :HD] = (dkk[keys, lanes] * SCALE).astype(BF16)
             grads[r // 2, r % 2, p, :, HD:] = dvv[keys, lanes].astype(BF16)
     grads_sibling(grads, rc, gsem).start()
+    chunk_dq(1024, jnp.full((1, TOK), mine, jnp.int32), kket, dst, d_ap, slice(TOK, 256))
     both(HeadSum.third, 1)
-    chunk_dq(8, jnp.full((1, TOK), mine, jnp.int32), kket, dst, d_p, slice(0, TOK))
     grads_second(grads, rc, gs, rg, gsem)
-    project(d_r.at[0:TOK], w, terms, 0, None)
-    both(HeadSum.first, 0)
-    project_early(d_p, w, early)
+    project(d_ap[...], w, put_ap, None, starts(0))
+    both(HeadSum.final, 1)
+    sums[1].write(out_r, TOK)
     both(HeadSum.second, 0)
-    grads_finish(gs, rg, gsem, d_p)
-    project_late(d_p, w, early, terms, 2)
-    both(HeadSum.first, 2)
+    grads_finish(gs, rg, gsem, late)
+    rows = late[...]
+    for offset in WEIGHT_ORDER:
+        for side, half in BLOCKS:
+            value = dot(w[offset, block_rows(side, half), 1024:], rows, NT)
+            terms[2, offset, half, side] = (early[offset, half, side] + value).astype(BF16)
+        if offset in (1, 3):
+            starts(2)[offset]()
     both(HeadSum.third, 0)
-    for half in range(2):
-        sums[1].final(half, out_r, TOK)
     both(HeadSum.second, 2)
-    for half in range(2):
-        sums[0].final(half, out_r, 0)
+    both(HeadSum.final, 0)
+    sums[0].write(out_r, 0)
     both(HeadSum.third, 2)
-    for half in range(2):
-        sums[2].final(half, out_p, 0)
+    both(HeadSum.final, 2)
+    sums[2].write(out_p, 0)
     grads_sibling(grads, rc, gsem).wait_send()
     for copy in grads_copies(gs, rg, gsem):
         copy.wait_send()
@@ -536,26 +566,31 @@
             VMEM((WIDE, 256), BF16),
             VMEM((WIDE, 256), BF16),
             VMEM((256, WIDE), BF16),
-            VMEM((1024, 256), BF16),
-            VMEM((1024, 256), BF16),
+            VMEM((3, 1024, 256), BF16),
+            VMEM((3, 1024, 256), BF16),
+            VMEM((WIDE, 256), F32),
+            VMEM((WIDE, 256), F32),
             VMEM((WIDE, 256), F32),
             VMEM((WIDE, 256), F32),
             VMEM((WIDE, 1024), BF16),
             VMEM((WIDE, 1024), BF16),
             VMEM((WIDE, 256), F32),
             VMEM((WIDE, 256), F32),
+            VMEM((TOK, 256), F32),
             VMEM((256, 256), F32),
+            VMEM((TOK, WIDE), BF16),
             VMEM((256, WIDE), BF16),
-            VMEM((TOK, WIDE), BF16),
+            VMEM((TOK, 256), BF16),
             VMEM((4, 2, 2, TOK, 256), BF16),
-            VMEM((4, TOK, WIDE), F32),
+            VMEM((4, 2, 2, HALF, TOK), F32),
             VMEM((4, WIDE, WIDE), BF16),
-            VMEM((3, 4, 2, TOK, COLS), BF16),
-            VMEM((3, 2, 2, 2, 64, COLS), BF16),
-            VMEM((3, 2, 2, 64, COLS), BF16),
-            VMEM((3, 2, 2, 64, COLS), BF16),
-            VMEM((3, 2, 64, COLS), BF16),
-            VMEM((3, 2, 64, COLS), BF16),
+            VMEM((3, 4, 2, 2, HALF, TOK), BF16),
+            VMEM((3, 2, 2, 2, HALF, TOK), BF16),
+            VMEM((3, 2, 2, HALF, TOK), BF16),
+            VMEM((3, 2, 2, HALF, TOK), BF16),
+            VMEM((3, 2, HALF, TOK), BF16),
+            VMEM((3, 2, HALF, TOK), BF16),
+            VMEM((3, COLS, TOK), F32),
             VMEM((4, 2, TOK, 256), BF16),
             VMEM((4, 2, TOK, 256), BF16),
             VMEM((7, TOK, 256), BF16),
@@ -565,7 +600,7 @@
             pltpu.SemaphoreType.DMA((8,)),
             pltpu.SemaphoreType.DMA((8,)),
             pltpu.SemaphoreType.DMA((4, 2, 3)),
-            pltpu.SemaphoreType.DMA((2, 3, 2, 3)),
+            pltpu.SemaphoreType.DMA((2, 3, 2, 5)),
             pltpu.SemaphoreType.DMA((2, 8)),
         ],
         compiler_params=pltpu.CompilerParams(

time: 92.5 us -> 71.5 us (0.77)
  Pallas kernels: 88.3 us -> 67.4 us
    pallas_call x1, Pallas kernels: 88.3 us -> 67.4 us  [shards(): pl.pallas_call(whole_kernel, out_shape=(jax.ShapeDtypeStruct((TOK, COLS),...]
where the time goes in v3:
time: 71.5 us; the launch traced here: 71.3 us
  Pallas kernels  67.4 us (94%)
  local copies, waits for them, and re-layouts  3.32 us (5%)
    pallas_call x1, Pallas kernels, shards(): pl.pallas_call(whole_kernel, out_shape=(jax.ShapeDtypeStruct((TOK, COLS),...  67.4 us
    unnamed x2, local copies, waits for them, and re-layouts  3.32 us

profile of v3, /device:TPU:0, one launch (start us, length us, event | category | flops | bytes accessed | tf_op | source)
XLA Modules:
  0.0 71.3 jit_solution(15431343130300749677)
XLA Ops:
  0.6 67.4 %attention_back.1 = (bf16[128,640]{1,0:T(8,128)(2,1)}, bf16[256,640]{1,0:T(8,128)(2,1)}) custom-call(s32[1,4]{1,0:T(1,128)} %lens_ref.1, s32[1,4]{1,0:T(1,128)} %prompt_ref.1, bf16[128,1024]{1,0:T(8,128)(2,1)} %q_p_h.1, bf16[128,128]{1,0:T(8,128)(2,1)} %k_p_h.1, bf16[128,128]{1,0:T(8,128)(2,1)} %v_p_h.1, bf16[128,1024]{1,0:T(8,128)(2,1)} %do_p_h.1, ...), custom_call_target="tpu_custom_call" | custom-call | tf_op jit(solution)/shard_map/attention_back/pallas_call | solution.py:550
  68.0 1.6 %copy.17 = bf16[128,640]{1,0:T(8,128)(2,1)} copy(bf16[128,640]{1,0:T(8,128)(2,1)} %get-tuple-element.4) | data formatting | bytes 327680
  69.6 1.7 %copy.18 = bf16[256,640]{1,0:T(8,128)(2,1)} copy(bf16[256,640]{1,0:T(8,128)(2,1)} %get-tuple-element.5) | data formatting | bytes 655360

commit v4 on v3

--- a/solution.py
+++ b/solution.py
@@ -52,7 +52,7 @@
     return n + 1 - 2 * lax.rem(n, 2)
 
 
-SEQ_STEPS = [(0, 1), (1, 0), (3, 0), (1, 1), (3, 1), (2, 0), (2, 1)]
+SEQ_STEPS = [(0, 1), (1, 0), (3, 0), (2, 0), (1, 1), (3, 1), (2, 1)]
 
 
 def head_peers():
@@ -67,13 +67,10 @@
 
 def gather_copies(kv, send, recv, fsend, frecv):
     n, head = lax.axis_index("seq"), lax.axis_index("head")
-    sib = seq_sibling()
-    firsts = [remote(kv.at[n], kv.at[n], fsend.at[0], frecv.at[0], sib, head)]
-    for j, (dy, dx) in enumerate(SEQ_STEPS):
-        firsts.append(
-            remote(kv.at[n], kv.at[n], send.at[j], recv.at[j], seq_peer(dy, dx), head)
-        )
-    return firsts
+    copies = [remote(kv.at[n], kv.at[n], fsend.at[0], frecv.at[0], seq_sibling(), head)]
+    for j, (dy, dx) in enumerate(SEQ_STEPS[:4]):
+        copies.append(remote(kv.at[n], kv.at[n], send.at[j], recv.at[j], seq_peer(dy, dx), head))
+    return copies
 
 
 def gather_start(kv, send, recv, fsend, frecv):
@@ -84,17 +81,26 @@
 def gather_finish(kv, send, recv, fsend, frecv):
     head = lax.axis_index("head")
     sib = seq_sibling()
-    firsts = gather_copies(kv, send, recv, fsend, frecv)
+    copies = gather_copies(kv, send, recv, fsend, frecv)
+    partner = seq_peer(0, 1)
+    copies[1].wait_recv()
+    for j, (dy, _) in enumerate(SEQ_STEPS[4:]):
+        passed = remote(
+            kv.at[partner], kv.at[partner], send.at[4 + j], recv.at[4 + j], seq_peer(dy, 0), head
+        )
+        passed.start()
+        copies.append(passed)
     forwards = []
     for j, (dy, dx) in enumerate(SEQ_STEPS):
         src = seq_peer(-dy, dx)
-        firsts[j + 1].wait_recv()
+        if j > 0:
+            copies[j + 1].wait_recv()
         forward = remote(kv.at[src], kv.at[src], fsend.at[j + 1], frecv.at[j + 1], sib, head)
         forward.start()
         forwards.append(forward)
-    for copy in [firsts[0]] + forwards:
+    for copy in [copies[0]] + forwards:
         copy.wait_recv()
-    for copy in firsts + forwards:
+    for copy in copies + forwards:
         copy.wait_send()
 
 
@@ -208,9 +214,9 @@
         top = next_top
 
 
-def chunk_product(keys, first, left, right, total):
-    for start, size in key_groups(keys):
-        span = slice(start, start + size)
+def chunk_product(low, high, first, left, right, total):
+    for start, size in key_groups(high - low):
+        span = slice(low + start, low + start + size)
         value = dot(left[span, :], right[...], NN)
         if first:
             total[span, :] = value
@@ -266,8 +272,10 @@
 
 
 class HeadSum:
-    def __init__(self, chunk, terms, r1, s2, r2, s3, r3, sums, sems):
+    def __init__(self, chunk, pieces, terms, r1, s2, r2, s3, r3, sums, sems):
         self.chunk = chunk
+        self.size = HALF // pieces
+        self.parts = [(half, piece) for piece in range(pieces) for half in range(2)]
         self.terms, self.r1, self.s2, self.r2, self.s3, self.r3 = (
             terms.at[chunk], r1.at[chunk], s2.at[chunk], r2.at[chunk], s3.at[chunk], r3.at[chunk]
         )
@@ -276,50 +284,71 @@
         self.seq = lax.axis_index("seq")
         self.z1, self.z3, self.flip = head_peers()
 
-    def copy(self, half, step):
-        send, recv = (self.sems.at[k, self.chunk, half, step] for k in range(2))
+    def rows(self, part):
+        return pl.ds(part[1] * self.size, self.size)
+
+    def copy(self, part, step):
+        half, piece = part
+        rows = self.rows(part)
+        send, recv = (self.sems.at[k, self.chunk, half, step, piece] for k in range(2))
         near, far = (self.z1, self.z3) if half == 0 else (self.z3, self.z1)
         if step < 2:
             side = 1 - step
             low, high = SIDES[half]["give"]
-            src = self.terms.at[pl.ds(low, high - low), half, side]
-            return remote(src, self.r1.at[half, side], send, recv, self.seq, near)
+            src = self.terms.at[pl.ds(low, high - low), half, side, rows]
+            return remote(src, self.r1.at[half, side, :, rows], send, recv, self.seq, near)
         if step < 4:
             k = step - 2
-            return remote(self.s2.at[half, k], self.r2.at[half, k], send, recv, self.seq, self.flip)
-        return remote(self.s3.at[half], self.r3.at[half], send, recv, self.seq, far)
+            return remote(
+                self.s2.at[half, k, rows], self.r2.at[half, k, rows], send, recv, self.seq, self.flip
+            )
+        return remote(self.s3.at[half, rows], self.r3.at[half, rows], send, recv, self.seq, far)
 
     def first(self, half):
-        self.copy(half, 0).start()
-        self.copy(half, 1).start()
-
-    def second(self, half):
-        self.copy(half, 0).wait_recv()
-        last = SIDES[half]["last"]
-        for k in (last, 1 - last):
-            offset = SIDES[half]["keep"][k]
-            total = self.terms[offset, half, 1].astype(F32) + self.r1[half, 1, k].astype(F32)
-            self.s2[half, k] = total.astype(BF16)
-            self.copy(half, 2 + k).start()
-
-    def kept(self, half, k):
-        self.copy(half, 2 + k).wait_recv()
+        for step in range(2):
+            for part in self.parts:
+                if part[0] == half:
+                    self.copy(part, step).start()
+
+    def cross(self, part, k):
+        half, rows = part[0], self.rows(part)
+        offset = SIDES[half]["keep"][k]
+        total = self.terms[offset, half, 1, rows].astype(F32) + self.r1[half, 1, k, rows].astype(F32)
+        self.s2[half, k, rows] = total.astype(BF16)
+        self.copy(part, 2 + k).start()
+
+    def second(self):
+        for part in self.parts:
+            self.copy(part, 0).wait_recv()
+            self.cross(part, SIDES[part[0]]["last"])
+        for part in self.parts:
+            self.cross(part, 1 - SIDES[part[0]]["last"])
+
+    def kept(self, part, k):
+        half, rows = part[0], self.rows(part)
+        self.copy(part, 2 + k).wait_recv()
         offset = SIDES[half]["keep"][k]
         return (
-            self.terms[offset, half, 0].astype(F32)
-            + self.r1[half, 0, k].astype(F32)
-            + self.r2[half, k].astype(F32)
+            self.terms[offset, half, 0, rows].astype(F32)
+            + self.r1[half, 0, k, rows].astype(F32)
+            + self.r2[half, k, rows].astype(F32)
         )
 
-    def third(self, half):
-        self.copy(half, 1).wait_recv()
-        self.s3[half] = self.kept(half, SIDES[half]["last"]).astype(BF16)
-        self.copy(half, 4).start()
-
-    def final(self, half):
-        total = self.kept(half, 1 - SIDES[half]["last"])
-        self.copy(half, 4).wait_recv()
-        self.sums[half * HALF : (half + 1) * HALF, :] = total + self.r3[half].astype(F32)
+    def third(self):
+        for part in self.parts:
+            self.copy(part, 1).wait_recv()
+            total = self.kept(part, SIDES[part[0]]["last"])
+            self.s3[part[0], self.rows(part)] = total.astype(BF16)
+            self.copy(part, 4).start()
+
+    def final(self):
+        for part in self.parts:
+            total = self.kept(part, 1 - SIDES[part[0]]["last"])
+            self.copy(part, 4).wait_recv()
+            start = part[0] * HALF + part[1] * self.size
+            self.sums[start : start + self.size, :] = total + self.r3[
+                part[0], self.rows(part)
+            ].astype(F32)
 
     def write(self, out, base):
         for part in range(5):
@@ -327,9 +356,9 @@
             out[base : base + TOK, lanes] = self.sums[lanes, :].T.astype(BF16)
 
     def drain(self):
-        for half in range(2):
+        for part in self.parts:
             for step in range(5):
-                self.copy(half, step).wait_send()
+                self.copy(part, step).wait_send()
 
 
 BLOCKS = ((1, 0), (1, 1), (0, 0), (0, 1))
@@ -340,20 +369,11 @@
     return slice(start, start + HALF)
 
 
-def project(rows, w, put, wait_weights, started):
-    for offset in WEIGHT_ORDER:
-        if wait_weights is not None:
-            wait_weights(offset)
-        for side, half in BLOCKS:
-            put(offset, half, side, dot(w[offset, block_rows(side, half), :], rows, NT))
-        if offset in started:
-            started[offset]()
-
-
-def grads_sibling(grads, rc, gsem):
+def grads_sibling(group, grads, rc, gsem):
     c = lax.rem(lax.axis_index("seq"), 2)
     return remote(
-        grads.at[:, 1 - c], rc, gsem.at[0, 7], gsem.at[1, 7], seq_sibling(), lax.axis_index("head")
+        grads.at[group, 1 - c], rc.at[group], gsem.at[0, 7 + group], gsem.at[1, 7 + group],
+        seq_sibling(), lax.axis_index("head"),
     )
 
 
@@ -375,8 +395,8 @@
 
 def grads_second(grads, rc, gs, rg, gsem):
     c = lax.rem(lax.axis_index("seq"), 2)
-    grads_sibling(grads, rc, gsem).wait_recv()
     for b in range(4):
+        grads_sibling(b, grads, rc, gsem).wait_recv()
         for p in range(2):
             gs[b, p] = (grads[b, c, p].astype(F32) + rc[b, p].astype(F32)).astype(BF16)
     for copy in grads_copies(gs, rg, gsem):
@@ -394,7 +414,7 @@
 
 def whole_kernel(
     lens_ref, prompt_ref, q_p_h, k_p_h, v_p_h, do_p_h, q_r_h, k_r_h, v_r_h, do_r_h, w_q, w_k, w_v,
-    out_p, out_r,
+    out,
     kv, q_p, do_p, q_r, do_r, k_r, v_r,
     kke, vve, kket, qext, doext, s0, s1, dp0, dp1, et, dst, dkk, dvv, bias0, bias1, d_b, d_ap, late, grads, early,
     w, terms, r1, s2, r2, s3, r3, totals, rc, gs, rg,
@@ -425,7 +445,7 @@
         copy.start()
     for copy in loads[2:]:
         copy.wait()
-    sums = [HeadSum(c, terms, r1, s2, r2, s3, r3, totals, hsem) for c in range(3)]
+    sums = [HeadSum(c, (1, 1, 2)[c], terms, r1, s2, r2, s3, r3, totals, hsem) for c in range(3)]
     mine = seq // 8
 
     row_prompts = []
@@ -459,7 +479,7 @@
             keys, bias_of, qext.at[chunk], doext.at[chunk], kke, vve, (s0, s1), (dp0, dp1), et, dst
         )
 
-    def response(half, first, d_ref):
+    def response(half, first):
         bias = (bias0, bias1)[half]
         keys = 1024 + (half + 1) * TOK
 
@@ -471,73 +491,79 @@
         scores(keys, local_bias, half)
         if first:
             turn_keys(kke, kket)
-        chunk_product(keys, first, et, doext.at[half], dvv)
-        chunk_product(keys, first, dst, qext.at[half], dkk)
-        chunk_dq(keys, row_prompts[half], kket, dst, d_ref, slice(0, TOK))
+        chunk_product(0, keys, first, et, doext.at[half], dvv)
+        chunk_product(0, keys, first, dst, qext.at[half], dkk)
+        rows = (d_ap, d_b)[half]
+        chunk_dq(keys, row_prompts[half], kket, dst, rows, slice(0, TOK))
         local = slice(1024 + half * TOK, 1024 + half * TOK + TOK)
-        d_ref[:TOK, 1024:1152] = ((dkk[local, :HD] + dkk[local, HD:]) * SCALE).astype(BF16)
-        d_ref[:TOK, 1152:] = (dvv[local, :HD] + dvv[local, HD:]).astype(BF16)
+        rows[:TOK, 1024:1152] = ((dkk[local, :HD] + dkk[local, HD:]) * SCALE).astype(BF16)
+        rows[:TOK, 1152:] = (dvv[local, :HD] + dvv[local, HD:]).astype(BF16)
 
     def wait_weights(offset):
         for copy in weight_copies((offset,), w_q, w_k, w_v, w, wsem):
             copy.wait()
 
-    def both(step, chunk):
-        for half in range(2):
-            step(sums[chunk], half)
-
-    def starts(chunk):
-        return {1: lambda: sums[chunk].first(0), 3: lambda: sums[chunk].first(1)}
-
-    def put_b(offset, half, side, value):
-        terms[1, offset, half, side] = value.astype(BF16)
-
-    def put_ap(offset, half, side, value):
-        terms[0, offset, half, side] = value[:, :TOK].astype(BF16)
-        early[offset, half, side] = value[:, TOK:]
-
-    response(1, True, d_b)
-    project(d_b[...], w, put_b, wait_weights, starts(1))
-    response(0, False, d_ap)
-    both(HeadSum.second, 1)
+    def start(chunk, offset):
+        if offset in (1, 3):
+            sums[chunk].first(offset // 2)
+
+    response(1, True)
+    for offset in WEIGHT_ORDER:
+        wait_weights(offset)
+        for side, half in BLOCKS:
+            value = dot(w[offset, block_rows(side, half), :], d_b[...], NT)
+            terms[1, offset, half, side] = value.astype(BF16)
+        start(1, offset)
+    response(0, False)
+    sums[1].second()
 
     scores(1024, lambda t, s: jnp.where(diff >= t * TOK, s, NEG), 2)
-    chunk_product(1024, False, et, doext.at[2], dvv)
-    chunk_product(1024, False, dst, qext.at[2], dkk)
-    for r in range(8):
-        keys = slice(r * TOK, (r + 1) * TOK)
-        for p in range(2):
-            lanes = slice(p * HD, (p + 1) * HD)
-            grads[r // 2, r % 2, p, :, :HD] = (dkk[keys, lanes] * SCALE).astype(BF16)
-            grads[r // 2, r % 2, p, :, HD:] = dvv[keys, lanes].astype(BF16)
-    grads_sibling(grads, rc, gsem).start()
+    for g in range(4):
+        chunk_product(g * 256, g * 256 + 256, False, et, doext.at[2], dvv)
+        chunk_product(g * 256, g * 256 + 256, False, dst, qext.at[2], dkk)
+        for r in range(2):
+            keys = slice(g * 256 + r * TOK, g * 256 + r * TOK + TOK)
+            for p in range(2):
+                lanes = slice(p * HD, (p + 1) * HD)
+                grads[g, r, p, :, :HD] = (dkk[keys, lanes] * SCALE).astype(BF16)
+                grads[g, r, p, :, HD:] = dvv[keys, lanes].astype(BF16)
+        grads_sibling(g, grads, rc, gsem).start()
     chunk_dq(1024, jnp.full((1, TOK), mine, jnp.int32), kket, dst, d_ap, slice(TOK, 256))
-    both(HeadSum.third, 1)
+    sums[1].third()
     grads_second(grads, rc, gs, rg, gsem)
-    project(d_ap[...], w, put_ap, None, starts(0))
-    both(HeadSum.final, 1)
-    sums[1].write(out_r, TOK)
-    both(HeadSum.second, 0)
-    grads_finish(gs, rg, gsem, late)
-    rows = late[...]
     for offset in WEIGHT_ORDER:
         for side, half in BLOCKS:
-            value = dot(w[offset, block_rows(side, half), 1024:], rows, NT)
+            value = dot(w[offset, block_rows(side, half), :], d_ap[...], NT)
+            terms[0, offset, half, side] = value[:, :TOK].astype(BF16)
+            early[offset, half, side] = value[:, TOK:]
+        start(0, offset)
+    sums[1].final()
+    sums[1].write(out, 2 * TOK)
+    sums[0].second()
+    grads_finish(gs, rg, gsem, late)
+    for offset in WEIGHT_ORDER:
+        for side, half in BLOCKS:
+            value = dot(w[offset, block_rows(side, half), 1024:], late[...], NT)
             terms[2, offset, half, side] = (early[offset, half, side] + value).astype(BF16)
-        if offset in (1, 3):
-            starts(2)[offset]()
-    both(HeadSum.third, 0)
-    both(HeadSum.second, 2)
-    both(HeadSum.final, 0)
-    sums[0].write(out_r, 0)
-    both(HeadSum.third, 2)
-    both(HeadSum.final, 2)
-    sums[2].write(out_p, 0)
-    grads_sibling(grads, rc, gsem).wait_send()
+        start(2, offset)
+    sums[0].third()
+    sums[2].second()
+    sums[0].final()
+    sums[0].write(out, TOK)
+    sums[2].third()
+    sums[2].final()
+    sums[2].write(out, 0)
+    for g in range(4):
+        grads_sibling(g, grads, rc, gsem).wait_send()
     for copy in grads_copies(gs, rg, gsem):
         copy.wait_send()
     for c in range(3):
         sums[c].drain()
+
+
+def split_kernel(both, out_p, out_r):
+    out_p[...] = both[:TOK, :]
+    out_r[...] = both[TOK:, :]
 
 
 def shards(
@@ -547,14 +573,11 @@
     whole = pl.BlockSpec(memory_space=VMEM)
     hbm = pl.BlockSpec(memory_space=pl.ANY)
     scalars = pl.BlockSpec(memory_space=pltpu.SMEM)
-    return pl.pallas_call(
+    both = pl.pallas_call(
         whole_kernel,
-        out_shape=(
-            jax.ShapeDtypeStruct((TOK, COLS), BF16),
-            jax.ShapeDtypeStruct((256, COLS), BF16),
-        ),
+        out_shape=jax.ShapeDtypeStruct((3 * TOK, COLS), BF16),
         in_specs=[scalars] * 2 + [hbm] * 11,
-        out_specs=(whole,) * 2,
+        out_specs=whole,
         scratch_shapes=[
             VMEM((16, 2, TOK, HD), BF16),
             VMEM((TOK, 1024), BF16),
@@ -600,8 +623,8 @@
             pltpu.SemaphoreType.DMA((8,)),
             pltpu.SemaphoreType.DMA((8,)),
             pltpu.SemaphoreType.DMA((4, 2, 3)),
-            pltpu.SemaphoreType.DMA((2, 3, 2, 5)),
-            pltpu.SemaphoreType.DMA((2, 8)),
+            pltpu.SemaphoreType.DMA((2, 3, 2, 5, 2)),
+            pltpu.SemaphoreType.DMA((2, 11)),
         ],
         compiler_params=pltpu.CompilerParams(
             collective_id=0, has_side_effects=True, vmem_limit_bytes=60 << 20
@@ -611,6 +634,16 @@
         resp_lengths, resp_prompt, q_prompt, k_prompt, v_prompt, do_prompt,
         q_resp, k_resp, v_resp, do_resp, w_query, w_key, w_value,
     )
+    return pl.pallas_call(
+        split_kernel,
+        out_shape=(
+            jax.ShapeDtypeStruct((TOK, COLS), BF16),
+            jax.ShapeDtypeStruct((2 * TOK, COLS), BF16),
+        ),
+        in_specs=[whole],
+        out_specs=(whole, whole),
+        name="split_rows",
+    )(both)
 
 
 def solution(mesh):

time: 71.5 us -> 68.5 us (0.958)
  local copies, waits for them, and re-layouts: 3.32 us -> 0 us
    unnamed x2 -> x0, local copies, waits for them, and re-layouts: 3.32 us -> none
    pallas_call x1 -> x2, Pallas kernels: 67.4 us -> 67.7 us  [the longest x1 65.9 us: shards(): pl.pallas_call(whole_kernel, out_shape=jax.ShapeDtypeStruct((3 * TOK, COL...]
where the time goes in v4:
time: 68.5 us; the launch traced here: 68.3 us
  Pallas kernels  67.7 us (99%)
    pallas_call x1, Pallas kernels, shards(): pl.pallas_call(whole_kernel, out_shape=jax.ShapeDtypeStruct((3 * TOK, COL...  65.9 us
    pallas_call x1, Pallas kernels, shards(): pl.pallas_call(split_kernel, out_shape=(jax.ShapeDtypeStruct((TOK, COLS),...  1.82 us

profile of v4, /device:TPU:0, one launch (start us, length us, event | category | flops | bytes accessed | tf_op | source)
XLA Modules:
  0.0 68.3 jit_solution(14359904924841514434)
XLA Ops:
  0.6 65.9 %attention_back.1.both = bf16[384,640]{1,0:T(8,128)(2,1)} custom-call(s32[1,4]{1,0:T(1,128)} %lens_ref.1, s32[1,4]{1,0:T(1,128)} %prompt_ref.1, bf16[128,1024]{1,0:T(8,128)(2,1)} %q_p_h.1, bf16[128,128]{1,0:T(8,128)(2,1)} %k_p_h.1, bf16[128,128]{1,0:T(8,128)(2,1)} %v_p_h.1, bf16[128,1024]{1,0:T(8,128)(2,1)} %do_p_h.1, bf16[256,1024]{1,0:T(8,128)(2,1)} %q_r_h.1, ...), custom_call_target="tpu_custom_call" | custom-call | tf_op jit(solution)/shard_map/attention_back/pallas_call | solution.py:576
  66.5 1.8 %split_rows.1 = (bf16[128,640]{1,0:T(8,128)(2,1)}, bf16[256,640]{1,0:T(8,128)(2,1)}) custom-call(bf16[384,640]{1,0:T(8,128)(2,1)} %attention_back.1.both), custom_call_target="tpu_custom_call" | custom-call | tf_op jit(solution)/shard_map/split_rows/pallas_call | solution.py:637

commit v5 on v4

--- a/solution.py
+++ b/solution.py
@@ -65,43 +65,61 @@
     return z1, z3, flip
 
 
-def gather_copies(kv, send, recv, fsend, frecv):
-    n, head = lax.axis_index("seq"), lax.axis_index("head")
-    copies = [remote(kv.at[n], kv.at[n], fsend.at[0], frecv.at[0], seq_sibling(), head)]
+def key_block(ref, n):
+    rows = pl.ds(pl.multiple_of(lax.rem(n, 8) * TOK, TOK), TOK)
+    lanes = pl.ds(pl.multiple_of(n // 8 * HD, HD), HD)
+    return ref.at[rows, lanes]
+
+
+def block_pair(keys, n, send, recv, slot, seq):
+    head = lax.axis_index("head")
+    return [
+        remote(key_block(ref, n), key_block(ref, n), send.at[slot, k], recv.at[slot, k], seq, head)
+        for k, ref in enumerate(keys)
+    ]
+
+
+def gather_pairs(keys, send, recv, fsend, frecv):
+    n = lax.axis_index("seq")
+    pairs = []
     for j, (dy, dx) in enumerate(SEQ_STEPS[:4]):
-        copies.append(remote(kv.at[n], kv.at[n], send.at[j], recv.at[j], seq_peer(dy, dx), head))
-    return copies
-
-
-def gather_start(kv, send, recv, fsend, frecv):
-    for copy in gather_copies(kv, send, recv, fsend, frecv):
+        pairs.append(block_pair(keys, n, send, recv, j, seq_peer(dy, dx)))
+    return pairs, block_pair(keys, n, fsend, frecv, 0, seq_sibling())
+
+
+def gather_start(keys, send, recv, fsend, frecv):
+    pairs, own = gather_pairs(keys, send, recv, fsend, frecv)
+    for pair in pairs:
+        for copy in pair:
+            copy.start()
+    for copy in own:
         copy.start()
 
 
-def gather_finish(kv, send, recv, fsend, frecv):
-    head = lax.axis_index("head")
-    sib = seq_sibling()
-    copies = gather_copies(kv, send, recv, fsend, frecv)
+def gather_finish(keys, send, recv, fsend, frecv):
+    pairs, own = gather_pairs(keys, send, recv, fsend, frecv)
     partner = seq_peer(0, 1)
-    copies[1].wait_recv()
     for j, (dy, _) in enumerate(SEQ_STEPS[4:]):
-        passed = remote(
-            kv.at[partner], kv.at[partner], send.at[4 + j], recv.at[4 + j], seq_peer(dy, 0), head
-        )
-        passed.start()
-        copies.append(passed)
-    forwards = []
-    for j, (dy, dx) in enumerate(SEQ_STEPS):
-        src = seq_peer(-dy, dx)
-        if j > 0:
-            copies[j + 1].wait_recv()
-        forward = remote(kv.at[src], kv.at[src], fsend.at[j + 1], frecv.at[j + 1], sib, head)
-        forward.start()
-        forwards.append(forward)
-    for copy in [copies[0]] + forwards:
-        copy.wait_recv()
-    for copy in copies + forwards:
-        copy.wait_send()
+        pairs.append(block_pair(keys, partner, send, recv, 4 + j, seq_peer(dy, 0)))
+    forwards = [
+        block_pair(keys, seq_peer(-dy, dx), fsend, frecv, j + 1, seq_sibling())
+        for j, (dy, dx) in enumerate(SEQ_STEPS)
+    ]
+    for k in range(2):
+        pairs[0][k].wait_recv()
+        for pair in pairs[4:]:
+            pair[k].start()
+    for j in range(7):
+        for k in range(2):
+            if j > 0:
+                pairs[j][k].wait_recv()
+            forwards[j][k].start()
+    for pair in [own] + forwards:
+        for copy in pair:
+            copy.wait_recv()
+    for pair in pairs + [own] + forwards:
+        for copy in pair:
+            copy.wait_send()
 
 
 def segment_of(place, lens_ref):
@@ -120,13 +138,7 @@
     return out
 
 
-def load_keys(kv, k_r, v_r, kke, vve):
-    for r in range(8):
-        rows = pl.ds(r * TOK, TOK)
-        kke[rows, :HD] = kv[r, 0]
-        kke[rows, HD:] = kv[8 + r, 0]
-        vve[rows, :HD] = kv[r, 1]
-        vve[rows, HD:] = kv[8 + r, 1]
+def load_keys(k_r, v_r, kke, vve):
     local = pl.ds(1024, 256)
     kke[local, :HD] = k_r[...]
     kke[local, HD:] = k_r[...]
@@ -304,11 +316,10 @@
             )
         return remote(self.s3.at[half, rows], self.r3.at[half, rows], send, recv, self.seq, far)
 
-    def first(self, half):
-        for step in range(2):
-            for part in self.parts:
-                if part[0] == half:
-                    self.copy(part, step).start()
+    def first(self, half, side):
+        for part in self.parts:
+            if part[0] == half:
+                self.copy(part, 1 - side).start()
 
     def cross(self, part, k):
         half, rows = part[0], self.rows(part)
@@ -361,7 +372,12 @@
                 self.copy(part, step).wait_send()
 
 
-BLOCKS = ((1, 0), (1, 1), (0, 0), (0, 1))
+GIVEN = (
+    ((2, 1, 0), (1, 1, 0)), ((2, 1, 1), (3, 1, 1)), ((2, 0, 0), (1, 0, 0)), ((2, 0, 1), (3, 0, 1)),
+)
+KEPT = (
+    (3, 1, 0), (0, 1, 0), (1, 1, 1), (0, 1, 1), (3, 0, 0), (0, 0, 0), (1, 0, 1), (0, 0, 1),
+)
 
 
 def block_rows(side, half):
@@ -415,7 +431,7 @@
 def whole_kernel(
     lens_ref, prompt_ref, q_p_h, k_p_h, v_p_h, do_p_h, q_r_h, k_r_h, v_r_h, do_r_h, w_q, w_k, w_v,
     out,
-    kv, q_p, do_p, q_r, do_r, k_r, v_r,
+    q_p, do_p, q_r, do_r, k_r, v_r,
     kke, vve, kket, qext, doext, s0, s1, dp0, dp1, et, dst, dkk, dvv, bias0, bias1, d_b, d_ap, late, grads, early,
     w, terms, r1, s2, r2, s3, r3, totals, rc, gs, rg,
     lsem, send, recv, fsend, frecv, wsem, hsem, gsem,
@@ -431,7 +447,7 @@
     loads = [
         pltpu.make_async_copy(src, dst_ref, lsem.at[k])
         for k, (src, dst_ref) in enumerate((
-            (k_p_h, kv.at[seq, 0]), (v_p_h, kv.at[seq, 1]), (q_r_h, q_r), (do_r_h, do_r),
+            (k_p_h, key_block(kke, seq)), (v_p_h, key_block(vve, seq)), (q_r_h, q_r), (do_r_h, do_r),
             (k_r_h, k_r), (v_r_h, v_r), (q_p_h, q_p), (do_p_h, do_p),
         ))
     ]
@@ -440,7 +456,7 @@
     for copy in loads[:2]:
         copy.wait()
     pl.semaphore_wait(barrier, len(seqs) + len(heads))
-    gather_start(kv, send, recv, fsend, frecv)
+    gather_start((kke, vve), send, recv, fsend, frecv)
     for copy in weight_copies(WEIGHT_ORDER, w_q, w_k, w_v, w, wsem):
         copy.start()
     for copy in loads[2:]:
@@ -471,8 +487,8 @@
         - lax.broadcasted_iota(jnp.int32, (TOK, 256), 0)
     )
     d_ap[TOK:, 1024:] = jnp.zeros((TOK, 256), BF16)
-    gather_finish(kv, send, recv, fsend, frecv)
-    load_keys(kv, k_r, v_r, kke, vve)
+    load_keys(k_r, v_r, kke, vve)
+    gather_finish((kke, vve), send, recv, fsend, frecv)
 
     def scores(keys, bias_of, chunk):
         chunk_scores(
@@ -493,6 +509,8 @@
             turn_keys(kke, kket)
         chunk_product(0, keys, first, et, doext.at[half], dvv)
         chunk_product(0, keys, first, dst, qext.at[half], dkk)
+        if not first:
+            sums[1].second()
         rows = (d_ap, d_b)[half]
         chunk_dq(keys, row_prompts[half], kket, dst, rows, slice(0, TOK))
         local = slice(1024 + half * TOK, 1024 + half * TOK + TOK)
@@ -503,19 +521,27 @@
         for copy in weight_copies((offset,), w_q, w_k, w_v, w, wsem):
             copy.wait()
 
-    def start(chunk, offset):
-        if offset in (1, 3):
-            sums[chunk].first(offset // 2)
+    def product(block, rows, low=0, high=WIDE):
+        offset, side, half = block
+        return dot(w[offset, block_rows(side, half), low:high], rows, NT)
+
+    def put(chunk, block, value):
+        offset, side, half = block
+        terms[chunk, offset, half, side] = value.astype(BF16)
+
+    def give(chunk, value_of):
+        for pair in GIVEN:
+            for block in pair:
+                put(chunk, block, value_of(block))
+            sums[chunk].first(pair[0][2], pair[0][1])
 
     response(1, True)
     for offset in WEIGHT_ORDER:
         wait_weights(offset)
-        for side, half in BLOCKS:
-            value = dot(w[offset, block_rows(side, half), :], d_b[...], NT)
-            terms[1, offset, half, side] = value.astype(BF16)
-        start(1, offset)
+    give(1, lambda block: product(block, d_b[...]))
+    for block in KEPT:
+        put(1, block, product(block, d_b[...]))
     response(0, False)
-    sums[1].second()
 
     scores(1024, lambda t, s: jnp.where(diff >= t * TOK, s, NEG), 2)
     for g in range(4):
@@ -531,21 +557,27 @@
     chunk_dq(1024, jnp.full((1, TOK), mine, jnp.int32), kket, dst, d_ap, slice(TOK, 256))
     sums[1].third()
     grads_second(grads, rc, gs, rg, gsem)
-    for offset in WEIGHT_ORDER:
-        for side, half in BLOCKS:
-            value = dot(w[offset, block_rows(side, half), :], d_ap[...], NT)
-            terms[0, offset, half, side] = value[:, :TOK].astype(BF16)
-            early[offset, half, side] = value[:, TOK:]
-        start(0, offset)
+    def joint(block):
+        value = product(block, d_ap[...])
+        offset, side, half = block
+        early[offset, half, side] = value[:, TOK:]
+        return value[:, :TOK]
+
+    give(0, joint)
+    for block in KEPT:
+        put(0, block, joint(block))
     sums[1].final()
     sums[1].write(out, 2 * TOK)
     sums[0].second()
     grads_finish(gs, rg, gsem, late)
-    for offset in WEIGHT_ORDER:
-        for side, half in BLOCKS:
-            value = dot(w[offset, block_rows(side, half), 1024:], late[...], NT)
-            terms[2, offset, half, side] = (early[offset, half, side] + value).astype(BF16)
-        start(2, offset)
+
+    def last(block):
+        offset, side, half = block
+        return early[offset, half, side] + product(block, late[...], 1024)
+
+    give(2, last)
+    for block in KEPT:
+        put(2, block, last(block))
     sums[0].third()
     sums[2].second()
     sums[0].final()
@@ -579,7 +611,6 @@
         in_specs=[scalars] * 2 + [hbm] * 11,
         out_specs=whole,
         scratch_shapes=[
-            VMEM((16, 2, TOK, HD), BF16),
             VMEM((TOK, 1024), BF16),
             VMEM((TOK, 1024), BF16),
             VMEM((256, 1024), BF16),
@@ -618,10 +649,10 @@
             VMEM((4, 2, TOK, 256), BF16),
             VMEM((7, TOK, 256), BF16),
             pltpu.SemaphoreType.DMA((8,)),
-            pltpu.SemaphoreType.DMA((7,)),
-            pltpu.SemaphoreType.DMA((7,)),
-            pltpu.SemaphoreType.DMA((8,)),
-            pltpu.SemaphoreType.DMA((8,)),
+            pltpu.SemaphoreType.DMA((7, 2)),
+            pltpu.SemaphoreType.DMA((7, 2)),
+            pltpu.SemaphoreType.DMA((8, 2)),
+            pltpu.SemaphoreType.DMA((8, 2)),
             pltpu.SemaphoreType.DMA((4, 2, 3)),
             pltpu.SemaphoreType.DMA((2, 3, 2, 5, 2)),
             pltpu.SemaphoreType.DMA((2, 11)),

time: 68.5 us -> 66.5 us (0.971)
  Pallas kernels: 67.7 us -> 65.7 us
    pallas_call x1, Pallas kernels: 65.9 us -> 63.9 us  [shards(): pl.pallas_call(whole_kernel, out_shape=jax.ShapeDtypeStruct((3 * TOK, COL...]
where the time goes in v5:
time: 66.5 us; the launch traced here: 66.3 us
  Pallas kernels  65.7 us (99%)
    pallas_call x1, Pallas kernels, shards(): pl.pallas_call(whole_kernel, out_shape=jax.ShapeDtypeStruct((3 * TOK, COL...  63.9 us
    pallas_call x1, Pallas kernels, shards(): pl.pallas_call(split_kernel, out_shape=(jax.ShapeDtypeStruct((TOK, COLS),...  1.82 us

profile of v5, /device:TPU:0, one launch (start us, length us, event | category | flops | bytes accessed | tf_op | source)
XLA Modules:
  0.0 66.3 jit_solution(1061241373016928191)
XLA Ops:
  0.6 63.9 %attention_back.1.both = bf16[384,640]{1,0:T(8,128)(2,1)} custom-call(s32[1,4]{1,0:T(1,128)} %lens_ref.1, s32[1,4]{1,0:T(1,128)} %prompt_ref.1, bf16[128,1024]{1,0:T(8,128)(2,1)} %q_p_h.1, bf16[128,128]{1,0:T(8,128)(2,1)} %k_p_h.1, bf16[128,128]{1,0:T(8,128)(2,1)} %v_p_h.1, bf16[128,1024]{1,0:T(8,128)(2,1)} %do_p_h.1, bf16[256,1024]{1,0:T(8,128)(2,1)} %q_r_h.1, ...), custom_call_target="tpu_custom_call" | custom-call | tf_op jit(solution)/shard_map/attention_back/pallas_call | solution.py:608
  64.5 1.8 %split_rows.1 = (bf16[128,640]{1,0:T(8,128)(2,1)}, bf16[256,640]{1,0:T(8,128)(2,1)}) custom-call(bf16[384,640]{1,0:T(8,128)(2,1)} %attention_back.1.both), custom_call_target="tpu_custom_call" | custom-call | tf_op jit(solution)/shard_map/split_rows/pallas_call | solution.py:668

commit v6 on v5

--- a/solution.py
+++ b/solution.py
@@ -566,9 +566,9 @@
     give(0, joint)
     for block in KEPT:
         put(0, block, joint(block))
+    sums[0].second()
     sums[1].final()
     sums[1].write(out, 2 * TOK)
-    sums[0].second()
     grads_finish(gs, rg, gsem, late)
 
     def last(block):

time: 66.5 us -> 66.5 us (level)
  no operation moved by 1% of the time
where the time goes in v6:
time: 66.5 us; the launch traced here: 66.3 us
  Pallas kernels  65.7 us (99%)
    pallas_call x1, Pallas kernels, shards(): pl.pallas_call(whole_kernel, out_shape=jax.ShapeDtypeStruct((3 * TOK, COL...  63.9 us
    pallas_call x1, Pallas kernels, shards(): pl.pallas_call(split_kernel, out_shape=(jax.ShapeDtypeStruct((TOK, COLS),...  1.82 us

profile of v6, /device:TPU:0, one launch (start us, length us, event | category | flops | bytes accessed | tf_op | source)
XLA Modules:
  0.0 66.3 jit_solution(10113291655955511751)
XLA Ops:
  0.6 63.9 %attention_back.1.both = bf16[384,640]{1,0:T(8,128)(2,1)} custom-call(s32[1,4]{1,0:T(1,128)} %lens_ref.1, s32[1,4]{1,0:T(1,128)} %prompt_ref.1, bf16[128,1024]{1,0:T(8,128)(2,1)} %q_p_h.1, bf16[128,128]{1,0:T(8,128)(2,1)} %k_p_h.1, bf16[128,128]{1,0:T(8,128)(2,1)} %v_p_h.1, bf16[128,1024]{1,0:T(8,128)(2,1)} %do_p_h.1, bf16[256,1024]{1,0:T(8,128)(2,1)} %q_r_h.1, ...), custom_call_target="tpu_custom_call" | custom-call | tf_op jit(solution)/shard_map/attention_back/pallas_call | solution.py:608
  64.5 1.8 %split_rows.1 = (bf16[128,640]{1,0:T(8,128)(2,1)}, bf16[256,640]{1,0:T(8,128)(2,1)}) custom-call(bf16[384,640]{1,0:T(8,128)(2,1)} %attention_back.1.both), custom_call_target="tpu_custom_call" | custom-call | tf_op jit(solution)/shard_map/split_rows/pallas_call | solution.py:668
